TPU v7x, 32 devices: a whole 2x2x4 slice. The times are simulated.
32 devices in a mesh: win: 8 (over z, y), var: 4 (over x, core).
Axes of the slice: x: 2, y: 2, z: 4, core: 2. Of those that a mesh axis runs over, the one named last changes fastest.
Arguments:
- inputs: bfloat16 [96, 256, 512], P('win', 'var'), may hold values from -6 to 6
- counts: int32 [96], P('win'), may hold values from 8 to 256, as said below
- row_index: int32 [96, 256], P('win'), may hold values from 0 to 255, each once within a row
- w_qkv: bfloat16 [2, 512, 1536], replicated, may hold values from -0.25 to 0.25
- bias_qv: float32 [2, 1024], replicated, may hold values from -2 to 2
- w_attn_out: bfloat16 [2, 512, 512], replicated, may hold values from -0.75 to 0.75
- out_bias: float32 [2, 2, 512], replicated, may hold values from -2 to 2
- w_in: bfloat16 [2, 512, 2048], replicated, may hold values from -0.25 to 0.25
- bias_in: float32 [2, 2048], replicated, may hold values from -2 to 2
- w_ffn_out: bfloat16 [2, 2048, 512], replicated, may hold values from -0.125 to 0.125
- norm_gain: float32 [2, 2, 512], replicated, may hold values from 0.5 to 1.5
- norm_bias: float32 [2, 2, 512], replicated, may hold values from -2 to 2
- cotangent: bfloat16 [96, 256, 512], P('win', 'var'), may hold values from -6 to 6
Outputs:
- layer_out: bfloat16 [96, 256, 512], P('win', 'var')
- grad_inputs: float32 [96, 256, 512], P('win', 'var')
- grad_qkv: float32 [2, 512, 1536], P(None, 'var')
- grad_bias_qv: float32 [2, 1024], P(None, 'var')
- grad_attn_out: float32 [2, 512, 512], P(None, 'var')
- grad_out_bias: float32 [2, 2, 512], P(None, None, 'var')
- grad_in: float32 [2, 512, 2048], P(None, 'var')
- grad_bias_in: float32 [2, 2048], P(None, 'var')
- grad_ffn_out: float32 [2, 2048, 512], P(None, 'var')
- grad_gain: float32 [2, 2, 512], P(None, None, 'var')
- grad_norm_bias: float32 [2, 2, 512], P(None, None, 'var')
Inputs may be any that keep to these rules, and one draw needn't show every extreme that they name: `counts`: in every aligned block of 12 windows one window has exactly 256 live variates. `row_index`: each window's list names every slot once; its first counts[w] entries are the live slots.
All inputs are finite; a program needn't handle non-finite values.
Results may differ from a plain program's by a relative error of at most 0.019.
Values may be sent and summed in bfloat16 or wider, within the bound.
A program may use at most 384 MiB of HBM per device.

v0:
```python
import functools

import jax
import jax.numpy as jnp
from jax import lax
from jax.experimental import pallas as pl
from jax.experimental.pallas import tpu as pltpu
from jax.sharding import PartitionSpec as P

HEADS = 8
LAYERS = 2


EPS = 1e-05
LOW = jnp.bfloat16
F32 = jnp.float32
MESH = pl.DeviceIdType.MESH
VMEM_BYTES = 60 << 20
PACKED = 448
SMOOTH = 0.7978845608028654
CUBIC = 0.044715


def layer_norm(values, gain, shift):
    centre = values - jnp.mean(values, axis=-1, keepdims=True)
    spread = jnp.mean(centre * centre, axis=-1, keepdims=True)
    return centre * lax.rsqrt(spread + EPS) * gain + shift


def smooth(values):
    return jax.nn.gelu(values, approximate=True)


def scores_of(query_heads, key_heads, key_valid, scale):
    raw = (
        jnp.einsum("wqhd,wkhd->whqk", query_heads, key_heads, preferred_element_type=jnp.float32)
        * scale
    )
    return jnp.where(key_valid[:, None, None, :], raw, -1e30)


def per_device(
    inputs,
    counts,
    row_index,
    w_qkv,
    bias_qv,
    w_attn_out,
    out_bias,
    w_in,
    bias_in,
    w_ffn_out,
    norm_gain,
    norm_bias,
    cotangent,
):
    wins, rows, width = inputs.shape
    cycle_size = lax.axis_size("var")
    length = rows * cycle_size
    first_row = lax.axis_index("var") * rows
    head_count = HEADS
    head_size = width // head_count
    scale = head_size ** (-0.5)
    flat = wins * rows
    slots = jnp.arange(length, dtype=jnp.int32)
    live = (slots[None, :] < counts[:, None]).astype(jnp.float32)
    window_ids = jnp.arange(wins, dtype=jnp.int32)[:, None]
    valid = jnp.zeros((wins, length), jnp.float32).at[window_ids, row_index].add(live)
    key_valid = valid > 0.5
    own_valid = lax.dynamic_slice_in_dim(valid, first_row, rows, 1).reshape(flat, 1)
    state = inputs.astype(jnp.float32).reshape(flat, width)
    kept = []
    for which_layer in range(LAYERS):
        x_low = state.astype(jnp.bfloat16)
        joint = jnp.dot(x_low, w_qkv[which_layer], preferred_element_type=jnp.float32)
        query = (joint[:, :width] + bias_qv[which_layer, :width]).astype(jnp.bfloat16)
        keys_low = joint[:, width : 2 * width].astype(jnp.bfloat16)
        values_low = (joint[:, 2 * width :] + bias_qv[which_layer, width:]).astype(jnp.bfloat16)
        pair = jnp.concatenate([keys_low, values_low], axis=1).reshape(wins, rows, 2 * width)
        whole = lax.all_gather(pair, "var", axis=1, tiled=True)
        query_heads = query.reshape(wins, rows, head_count, head_size)
        key_heads = whole[:, :, :width].reshape(wins, length, head_count, head_size)
        value_heads = whole[:, :, width:].reshape(wins, length, head_count, head_size)
        scores = scores_of(query_heads, key_heads, key_valid, scale)
        peak = jnp.max(scores, axis=-1, keepdims=True)
        expo = jnp.exp(scores - peak)
        total = jnp.sum(expo, axis=-1, keepdims=True)
        probs = expo / total
        top = peak + jnp.log(total)
        mixed = (
            jnp.einsum(
                "whqk,wkhd->wqhd",
                probs.astype(jnp.bfloat16),
                value_heads,
                preferred_element_type=jnp.float32,
            )
            .reshape(flat, width)
            .astype(jnp.bfloat16)
        )
        attn = (
            jnp.dot(mixed, w_attn_out[which_layer], preferred_element_type=jnp.float32)
            + out_bias[which_layer, 0]
        )
        normed, norm_one = jax.vjp(
            layer_norm, state + attn, norm_gain[which_layer, 0], norm_bias[which_layer, 0]
        )
        normed_low = normed.astype(jnp.bfloat16)
        hidden = (
            jnp.dot(normed_low, w_in[which_layer], preferred_element_type=jnp.float32)
            + bias_in[which_layer]
        )
        active, gelu_back = jax.vjp(smooth, hidden)
        active_low = active.astype(jnp.bfloat16)
        ffn = (
            jnp.dot(active_low, w_ffn_out[which_layer], preferred_element_type=jnp.float32)
            + out_bias[which_layer, 1]
        )
        state, norm_two = jax.vjp(
            layer_norm, normed + ffn, norm_gain[which_layer, 1], norm_bias[which_layer, 1]
        )
        stored = whole
        kept.append(
            (
                x_low,
                query_heads,
                stored,
                top,
                mixed,
                norm_one,
                normed_low,
                gelu_back,
                active_low,
                norm_two,
            )
        )
    layer_out = (state * own_valid).astype(jnp.bfloat16).reshape(wins, rows, width)
    grad = cotangent.astype(jnp.float32).reshape(flat, width) * own_valid
    collected = []
    for which_layer in reversed(range(LAYERS)):
        (
            x_low,
            query_heads,
            stored,
            top,
            mixed,
            norm_one,
            normed_low,
            gelu_back,
            active_low,
            norm_two,
        ) = kept[which_layer]
        dz_two, gain_two, shift_two = norm_two(grad)
        d_ffn = dz_two.astype(jnp.bfloat16)
        g_ffn_out = jnp.einsum("rf,rd->fd", active_low, d_ffn, preferred_element_type=jnp.float32)
        bias_two = jnp.sum(d_ffn.astype(jnp.float32), axis=0)
        d_active = jnp.einsum(
            "rd,fd->rf", d_ffn, w_ffn_out[which_layer], preferred_element_type=jnp.float32
        )
        (d_hidden,) = gelu_back(d_active)
        d_hidden = d_hidden.astype(jnp.bfloat16)
        g_in = jnp.einsum("rd,rf->df", normed_low, d_hidden, preferred_element_type=jnp.float32)
        g_bias_in = jnp.sum(d_hidden.astype(jnp.float32), axis=0)
        d_normed = dz_two + jnp.einsum(
            "rf,df->rd", d_hidden, w_in[which_layer], preferred_element_type=jnp.float32
        )
        dz_one, gain_one, shift_one = norm_one(d_normed)
        d_attn = dz_one.astype(jnp.bfloat16)
        g_attn_out = jnp.einsum("re,rd->ed", mixed, d_attn, preferred_element_type=jnp.float32)
        bias_one = jnp.sum(d_attn.astype(jnp.float32), axis=0)
        d_mixed = jnp.einsum(
            "rd,ed->re", d_attn, w_attn_out[which_layer], preferred_element_type=jnp.float32
        ).astype(jnp.bfloat16)
        whole = stored
        key_heads = whole[:, :, :width].reshape(wins, length, head_count, head_size)
        value_heads = whole[:, :, width:].reshape(wins, length, head_count, head_size)
        scores = scores_of(query_heads, key_heads, key_valid, scale)
        probs = jnp.exp(scores - top)
        grad_heads = d_mixed.reshape(wins, rows, head_count, head_size)
        d_probs = jnp.einsum(
            "wqhd,wkhd->whqk", grad_heads, value_heads, preferred_element_type=jnp.float32
        )
        centre = jnp.sum(probs * d_probs, axis=-1, keepdims=True)
        d_scores = (probs * (d_probs - centre)).astype(jnp.bfloat16)
        probs_low = probs.astype(jnp.bfloat16)
        d_query = (
            jnp.einsum("whqk,wkhd->wqhd", d_scores, key_heads, preferred_element_type=jnp.float32)
            * scale
        )
        d_query = d_query.reshape(flat, width).astype(jnp.bfloat16)
        span_rows = lax.axis_size("var") * rows
        d_key = (
            jnp.einsum("whqk,wqhd->kwhd", d_scores, query_heads, preferred_element_type=jnp.float32)
            * scale
        )
        d_value = jnp.einsum(
            "whqk,wqhd->kwhd", probs_low, grad_heads, preferred_element_type=jnp.float32
        )
        key_grads = lax.psum_scatter(
            jnp.concatenate(
                [d_key.reshape(span_rows, wins, width), d_value.reshape(span_rows, wins, width)],
                axis=2,
            ).astype(jnp.bfloat16),
            "var",
            scatter_dimension=0,
            tiled=True,
        ).astype(jnp.float32)
        key_grads = (
            jnp.transpose(key_grads, (1, 0, 2)).reshape(flat, 2 * width).astype(jnp.bfloat16)
        )
        d_joint = jnp.concatenate([d_query, key_grads], axis=1)
        g_qkv = jnp.einsum("rd,re->de", x_low, d_joint, preferred_element_type=jnp.float32)
        g_bias_qv = jnp.concatenate(
            [
                jnp.sum(d_query.astype(jnp.float32), axis=0),
                jnp.sum(key_grads[:, width:].astype(jnp.float32), axis=0),
            ]
        )
        grad = dz_one + jnp.einsum(
            "re,de->rd", d_joint, w_qkv[which_layer], preferred_element_type=jnp.float32
        )
        g_out_bias = jnp.stack([bias_one, bias_two])
        g_gain = jnp.stack([gain_one, gain_two])
        g_shift = jnp.stack([shift_one, shift_two])
        terms = (
            g_qkv,
            g_bias_qv,
            g_attn_out,
            g_out_bias,
            g_in,
            g_bias_in,
            g_ffn_out,
            g_gain,
            g_shift,
        )
        collected.append(terms)
    collected = collected[::-1]
    stacked = tuple((jnp.stack([entry[position] for entry in collected]) for position in range(9)))
    shards = (
        lax.psum_scatter(
            stacked[0].astype(jnp.bfloat16), "var", scatter_dimension=1, tiled=True
        ).astype(jnp.float32),
        lax.psum_scatter(
            stacked[1].astype(jnp.bfloat16), "var", scatter_dimension=1, tiled=True
        ).astype(jnp.float32),
        lax.psum_scatter(
            stacked[2].astype(jnp.bfloat16), "var", scatter_dimension=1, tiled=True
        ).astype(jnp.float32),
        lax.psum_scatter(
            stacked[3].astype(jnp.bfloat16), "var", scatter_dimension=2, tiled=True
        ).astype(jnp.float32),
        lax.psum_scatter(
            stacked[4].astype(jnp.bfloat16), "var", scatter_dimension=1, tiled=True
        ).astype(jnp.float32),
        lax.psum_scatter(
            stacked[5].astype(jnp.bfloat16), "var", scatter_dimension=1, tiled=True
        ).astype(jnp.float32),
        lax.psum_scatter(
            stacked[6].astype(jnp.bfloat16), "var", scatter_dimension=1, tiled=True
        ).astype(jnp.float32),
        lax.psum_scatter(
            stacked[7].astype(jnp.bfloat16), "var", scatter_dimension=2, tiled=True
        ).astype(jnp.float32),
        lax.psum_scatter(
            stacked[8].astype(jnp.bfloat16), "var", scatter_dimension=2, tiled=True
        ).astype(jnp.float32),
    )
    stacked = (
        lax.psum(shards[0].astype(jnp.bfloat16), "win").astype(jnp.float32),
        lax.psum(shards[1].astype(jnp.bfloat16), "win").astype(jnp.float32),
        lax.psum(shards[2].astype(jnp.bfloat16), "win").astype(jnp.float32),
        lax.psum(shards[3].astype(jnp.bfloat16), "win").astype(jnp.float32),
        lax.psum(shards[4].astype(jnp.bfloat16), "win").astype(jnp.float32),
        lax.psum(shards[5].astype(jnp.bfloat16), "win").astype(jnp.float32),
        lax.psum(shards[6].astype(jnp.bfloat16), "win").astype(jnp.float32),
        lax.psum(shards[7].astype(jnp.bfloat16), "win").astype(jnp.float32),
        lax.psum(shards[8].astype(jnp.bfloat16), "win").astype(jnp.float32),
    )
    grad_inputs = grad.reshape(wins, rows, width)
    return (
        layer_out,
        grad_inputs,
        stacked[0],
        stacked[1],
        stacked[2],
        stacked[3],
        stacked[4],
        stacked[5],
        stacked[6],
        stacked[7],
        stacked[8],
    )


def dot(left, right, left_dim, right_dim):
    return lax.dot_general(
        left, right, (((left_dim,), (right_dim,)), ((), ())), preferred_element_type=F32
    )


def flip(index, bit):
    return index + bit - 2 * bit * lax.rem(index // bit, 2)


def half_of(index, bit):
    return lax.rem(index // bit, 2)


def partner(axis, bit):
    win, var = lax.axis_index("win"), lax.axis_index("var")
    if axis == "win":
        return (flip(win, bit), var)
    return (win, flip(var, bit))


def greet(partners):
    barrier = pltpu.get_barrier_semaphore()
    for other in partners:
        pl.semaphore_signal(barrier, inc=1, device_id=other, device_id_type=MESH)
    pl.semaphore_wait(barrier, len(partners))


def assign(counts, wins, owners):
    each = wins // owners
    keys = [counts[w] * wins + w for w in range(wins)]
    for stop in range(wins - 1, 0, -1):
        for low in range(stop):
            first, second = keys[low], keys[low + 1]
            keys[low], keys[low + 1] = jnp.maximum(first, second), jnp.minimum(first, second)
    load = [jnp.int32(0)] * owners
    held = [jnp.int32(0)] * owners
    slots, names = [], []
    for key in keys:
        count, name = key // wins, lax.rem(key, wins)
        best, which = load[0] + (held[0] // each) * 1000000, jnp.int32(0)
        for owner in range(1, owners):
            price = load[owner] + (held[owner] // each) * 1000000
            better = price < best
            best = jnp.where(better, price, best)
            which = jnp.where(better, owner, which)
        slot = jnp.int32(0)
        for owner in range(owners):
            mine = which == owner
            slot = jnp.where(mine, owner * each + held[owner], slot)
            load[owner] = jnp.where(mine, load[owner] + ((count + 15) // 16) * 16, load[owner])
            held[owner] = jnp.where(mine, held[owner] + 1, held[owner])
        slots.append(slot)
        names.append(name)
    order = []
    for place in range(wins):
        window = jnp.int32(0)
        for slot, name in zip(slots, names):
            window = jnp.where(slot == place, name, window)
        order.append(window)
    return order


def spread_kernel(
    owners, counts, x, x_out, meta, x_stage, x_send, x_recv, own_sem
):
    wins, rows = x.shape[0], x.shape[1]
    each = wins // owners
    me, win = lax.axis_index("var"), lax.axis_index("win")
    others = [flip(me, 1), flip(me, 2), flip(flip(me, 1), 2)]
    barrier = pltpu.get_barrier_semaphore()
    for other in others:
        pl.semaphore_signal(barrier, inc=1, device_id=(win, other), device_id_type=MESH)
    order = assign(counts, wins, owners)
    for place in range(wins):
        meta[place] = order[place]
        x_stage[place] = x[order[place]]
    pl.semaphore_wait(barrier, len(others))

    sent = []
    for place, other in enumerate(others):
        sent.append(
            pltpu.make_async_remote_copy(
                src_ref=x_stage.at[pl.ds(other * each, each)],
                dst_ref=x_out.at[:, pl.ds(pl.multiple_of(me * rows, rows), rows), :],
                send_sem=x_send.at[place],
                recv_sem=x_recv.at[place],
                device_id=(win, other),
                device_id_type=MESH,
            )
        )
    for copy in sent:
        copy.start()
    own = pl.ds(pl.multiple_of(me * rows, rows), rows)
    own_x = pltpu.make_async_copy(x_stage.at[pl.ds(me * each, each)], x_out.at[:, own, :], own_sem)
    own_x.start()
    padded = jnp.int32(0)
    for place in range(each):
        name = jnp.int32(0)
        for owner in range(owners):
            name = jnp.where(me == owner, order[owner * each + place], name)
        meta[wins + place] = name
        meta[wins + each + place] = counts[name]
        padded = padded + ((counts[name] + 15) // 16) * 16
    meta[wins + 2 * each] = me
    meta[wins + 2 * each + 1] = padded

    own_x.wait()
    for copy in sent:
        copy.wait()


class Plan:
    def __init__(self, meta, wins, each):
        self.names = [meta[wins + place] for place in range(each)]
        self.counts = [meta[wins + each + place] for place in range(each)]
        self.starts = []
        total = jnp.int32(0)
        for count in self.counts:
            self.starts.append(total)
            total = total + ((count + 15) // 16) * 16
        self.total = total
        self.blocks = (total + 127) // 128

    def each_block(self, body):
        def step(block, carry):
            body(128, block, pl.ds(pl.multiple_of(block * 128, 128), 128))
            return carry

        lax.fori_loop(0, self.blocks, step, 0)

    def pick(self, values, window):
        chosen = values[0]
        for place in range(1, len(values)):
            chosen = jnp.where(window == place, values[place], chosen)
        return chosen

    def each_window(self, body):
        def step(window, carry):
            count = self.pick(self.counts, window)
            start = pl.multiple_of(self.pick(self.starts, window), 16)
            body(256, count, pl.ds(start, 256))

            return carry

        lax.fori_loop(0, len(self.counts), step, 0)


def marks(row_index, name, count, length):
    listed = row_index[pl.ds(name, 1), :]
    slot = lax.broadcasted_iota(jnp.int32, (length, length), 0)
    place = lax.broadcasted_iota(jnp.int32, (length, length), 1)
    hit = jnp.logical_and(slot == listed, place < count)
    return jnp.where(hit, 1.0, 0.0).astype(LOW)


def mean_of(values):
    return jnp.mean(values, axis=-1, keepdims=True)


def normalize(values):
    centre = values - mean_of(values)
    inverse = lax.rsqrt(mean_of(centre * centre) + EPS)
    return centre * inverse, inverse


def normalize_back(grad, gain, normal, inverse):
    scaled = grad * gain
    return inverse * (scaled - mean_of(scaled) - normal * mean_of(scaled * normal))


def two_heads(pair, lane_low, lane_high):
    return jnp.concatenate([pair * lane_low, pair * lane_high], axis=0)


def lane_masks(lanes):
    lane = lax.broadcasted_iota(jnp.int32, (1, lanes), 1)
    low = jnp.where(lane < lanes // 2, 1.0, 0.0)
    return low.astype(LOW), (1.0 - low).astype(LOW)


def join_heads(stacked):
    size, lanes = stacked.shape[0] // 2, stacked.shape[1]
    lane = lax.broadcasted_iota(jnp.int32, (size, lanes), 1)
    return jnp.where(lane < lanes // 2, stacked[:size], stacked[size:])


def forward_kernel(
    meta, row_index, x, w_qkv, w_attn, w_in, w_out, bias_qv, out_bias, bias_in, gain, shift,
    lefts_out, qkv_out, slope_out, normal_out, inverse_out, top_out, layer_out,
    wv_qkv, wv_attn, wv_in, wv_out, lefts, qkv, slope, normal, inverse, top, state,
    weight_sem, out_sem,
):
    each, length, width = x.shape
    wins = row_index.shape[0]
    layers = w_qkv.shape[0]
    hidden_width = w_in.shape[2]
    pieces = hidden_width // width
    part = width // pieces
    plan = Plan(meta, wins, each)
    weights = ((w_qkv, wv_qkv), (w_attn, wv_attn), (w_in, wv_in), (w_out, wv_out))

    def fetch(layer, which):
        source, target = weights[which]
        return pltpu.make_async_copy(
            source.at[layer], target.at[layer], weight_sem.at[layer, which]
        )

    for layer in range(layers):
        for which in range(4):
            fetch(layer, which).start()

    state[...] = jnp.zeros_like(state)
    for layer in range(layers):
        lefts[layer, 1] = jnp.zeros(lefts.shape[2:], LOW)
        qkv[layer] = jnp.zeros(qkv.shape[1:], LOW)
    for place in range(each):
        hits = marks(row_index, plan.names[place], plan.counts[place], length)
        start = pl.multiple_of(plan.starts[place], 16)
        state[pl.ds(start, length), :] = dot(hits, x[place], 0, 0)

    kept = (
        (lefts, lefts_out, lambda ref, layer, rows: ref.at[layer, :, rows, :]),
        (qkv, qkv_out, lambda ref, layer, rows: ref.at[layer, rows, :]),
        (slope, slope_out, lambda ref, layer, rows: ref.at[layer, rows, :]),
        (normal, normal_out, lambda ref, layer, rows: ref.at[layer, :, rows, :]),
        (inverse, inverse_out, lambda ref, layer, rows: ref.at[layer, rows, :]),
        (top, top_out, lambda ref, layer, rows: ref.at[layer, rows, :]),
    )

    def stores(layer, block, rows):
        return [
            pltpu.make_async_copy(
                view(source, layer, rows), view(target, layer, rows), out_sem.at[layer, which, block]
            )
            for which, (source, target, view) in enumerate(kept)
        ]

    lane_low, lane_high = lane_masks(128)

    def one_layer(layer, carry):
        fetch(layer, 0).wait()

        def project(size, block, rows):
            tokens = state[rows, :].astype(LOW)
            lefts[layer, 0, rows, :] = tokens
            for which in range(3):
                columns = slice(which * width, (which + 1) * width)
                joint = dot(tokens, wv_qkv[layer, :, columns], 1, 0)
                if which == 0:
                    joint = (joint + bias_qv[pl.ds(layer, 1), :width]).astype(LOW) * LOW(0.125)
                elif which == 2:
                    joint = (joint + bias_qv[pl.ds(layer, 1), width:]).astype(LOW)
                else:
                    joint = joint.astype(LOW)
                qkv[layer, rows, columns] = joint

        plan.each_block(project)

        def attend(size, count, rows):
            column = lax.broadcasted_iota(jnp.int32, (2 * size, size), 1)
            live = column < count

            def pair(which, carry):
                at = pl.multiple_of(which * 128, 128)
                query = two_heads(qkv[layer, rows, pl.ds(at, 128)], lane_low, lane_high)
                key = qkv[layer, rows, pl.ds(pl.multiple_of(at + width, 128), 128)]
                value = qkv[layer, rows, pl.ds(pl.multiple_of(at + 2 * width, 128), 128)]
                scores = jnp.where(live, dot(query, key, 1, 1), -1e30)
                peak = jnp.max(scores, axis=-1, keepdims=True)
                expo = jnp.exp(scores - peak)
                total = jnp.sum(expo, axis=-1, keepdims=True)
                probs = (expo * (1.0 / total)).astype(LOW)
                lefts[layer, 1, rows, pl.ds(at, 128)] = join_heads(dot(probs, value, 1, 0)).astype(LOW)
                logs = jnp.broadcast_to(peak + jnp.log(total), (2 * size, 128))
                top[layer, rows, pl.ds(at, 128)] = join_heads(logs)
                return carry

            lax.fori_loop(0, width // 128, pair, 0)

        plan.each_window(attend)
        for which in range(1, 4):
            fetch(layer, which).wait()

        def feed(size, block, rows):
            first = dot(lefts[layer, 1, rows, :], wv_attn[layer], 1, 0) + out_bias[layer, 0:1, :]
            one, inverse_one = normalize(state[rows, :] + first)
            normal[layer, 0, rows, :] = one
            after = one * gain[layer, 0:1, :] + shift[layer, 0:1, :]
            after_low = after.astype(LOW)
            lefts[layer, 2, rows, :] = after_low
            second = jnp.zeros((size, width), F32)
            for piece in range(pieces):
                columns = slice(piece * width, (piece + 1) * width)
                hidden = dot(after_low, wv_in[layer, :, columns], 1, 0) + bias_in[pl.ds(layer, 1), columns]
                squared = hidden * hidden
                bend = jnp.tanh(SMOOTH * hidden * (1.0 + CUBIC * squared))
                half = 0.5 * (1.0 + bend)
                active = (hidden * half).astype(LOW)
                rise = half + 0.5 * hidden * (1.0 - bend * bend) * (
                    SMOOTH * (1.0 + 3.0 * CUBIC * squared)
                )
                slope[layer, rows, columns] = rise.astype(LOW)
                for sub in range(pieces):
                    lefts[layer, 3 + sub, rows, piece * part : (piece + 1) * part] = active[
                        :, sub * part : (sub + 1) * part
                    ]
                second = second + dot(active, wv_out[layer, columns, :], 1, 0)
            two, inverse_two = normalize(after + second + out_bias[layer, 1:2, :])
            normal[layer, 1, rows, :] = two
            state[rows, :] = two * gain[layer, 1:2, :] + shift[layer, 1:2, :]
            lane = lax.broadcasted_iota(jnp.int32, (size, 128), 1)
            inverse[layer, rows, :] = jnp.where(lane < 64, inverse_one, inverse_two)
            for copy in stores(layer, block, rows):
                copy.start()

        plan.each_block(feed)
        return carry

    lax.fori_loop(0, layers, one_layer, 0)
    for place in range(each):
        hits = marks(row_index, plan.names[place], plan.counts[place], length)
        start = pl.multiple_of(plan.starts[place], 16)
        layer_out[place] = dot(hits, state[pl.ds(start, length), :].astype(LOW), 1, 0).astype(LOW)

    for layer in range(layers):

        def finish(size, block, rows, layer=layer):
            for copy in stores(layer, block, rows):
                copy.wait()

        plan.each_block(finish)


def backward_kernel(
    meta, row_index, g, w_qkv, w_attn, w_in, w_out, gain,
    qkv_in, slope_in, normal_in, inverse_in, top_in,
    rights_out, grad_out, sums,
    wv_qkv, wv_attn, wv_in, wv_out, rights, qkv, slope, normal, inverse, top, state, mixed_grad,
    weight_sem, in_sem, out_sem,
):
    each, length, width = g.shape
    wins = row_index.shape[0]
    layers = w_qkv.shape[0]
    hidden_width = w_in.shape[2]
    pieces = hidden_width // width
    plan = Plan(meta, wins, each)
    weights = ((w_out, wv_out), (w_in, wv_in), (w_attn, wv_attn), (w_qkv, wv_qkv))

    def fetch(layer, which):
        source, target = weights[which]
        return pltpu.make_async_copy(
            source.at[layer], target.at[layer], weight_sem.at[layer, which]
        )

    kept = (
        (normal_in, normal, lambda ref, layer, rows: ref.at[layer, :, rows, :]),
        (inverse_in, inverse, lambda ref, layer, rows: ref.at[layer, rows, :]),
        (slope_in, slope, lambda ref, layer, rows: ref.at[layer, rows, :]),
        (qkv_in, qkv, lambda ref, layer, rows: ref.at[layer, rows, :]),
        (top_in, top, lambda ref, layer, rows: ref.at[layer, rows, :]),
    )

    def loads(layer, block, rows):
        return [
            pltpu.make_async_copy(
                view(source, layer, rows), view(target, layer, rows), in_sem.at[layer, which, block]
            )
            for which, (source, target, view) in enumerate(kept)
        ]

    for layer in range(layers):
        qkv[layer, 128:] = jnp.zeros((qkv.shape[1] - 128, qkv.shape[2]), LOW)
    for layer in reversed(range(layers)):

        def begin(size, block, rows, layer=layer):
            for copy in loads(layer, block, rows):
                copy.start()

        fetch(layer, 0).start()
        plan.each_block(begin)
        for which in range(1, 4):
            fetch(layer, which).start()

    state[...] = jnp.zeros_like(state)
    mixed_grad[...] = jnp.zeros_like(mixed_grad)
    sums[...] = jnp.zeros_like(sums)
    for layer in range(layers):
        rights[layer, 0:3] = jnp.zeros((3,) + rights.shape[2:], LOW)
    for place in range(each):
        hits = marks(row_index, plan.names[place], plan.counts[place], length)
        start = pl.multiple_of(plan.starts[place], 16)
        state[pl.ds(start, length), :] = dot(hits, g[place], 0, 0)

    lane_low, lane_high = lane_masks(128)

    def add_rows(layer, place, values):
        sums[layer, place : place + 1, :] += jnp.sum(values, axis=0, keepdims=True)

    def one_layer(step, carry):
        layer = layers - 1 - step
        for which in range(3):
            fetch(layer, which).wait()

        def feed(size, block, rows):
            for copy in loads(layer, block, rows):
                copy.wait()
            grad = state[rows, :]
            two = normal[layer, 1, rows, :]
            add_rows(layer, 9, grad * two)
            add_rows(layer, 11, grad)
            back = normalize_back(grad, gain[layer, 1:2, :], two, inverse[layer, rows, 64:65])
            back_low = back.astype(LOW)
            rights[layer, 8, rows, :] = back_low
            add_rows(layer, 3, back_low.astype(F32))
            for piece in range(pieces):
                columns = slice(piece * width, (piece + 1) * width)
                active = dot(back_low, wv_out[layer, columns, :], 1, 1)
                hidden = (active * slope[layer, rows, columns].astype(F32)).astype(LOW)
                rights[layer, 4 + piece, rows, :] = hidden
                add_rows(layer, 4 + piece, hidden.astype(F32))
                back = back + dot(hidden, wv_in[layer, :, columns], 1, 1)
            one = normal[layer, 0, rows, :]
            add_rows(layer, 8, back * one)
            add_rows(layer, 10, back)
            back = normalize_back(back, gain[layer, 0:1, :], one, inverse[layer, rows, 0:1])
            back_low = back.astype(LOW)
            rights[layer, 3, rows, :] = back_low
            add_rows(layer, 2, back_low.astype(F32))
            mixed_grad[rows, :] = dot(back_low, wv_attn[layer], 1, 1).astype(LOW)
            state[rows, :] = back

        plan.each_block(feed)

        def attend(size, count, rows):
            row = lax.broadcasted_iota(jnp.int32, (2 * size, size), 0)
            column = lax.broadcasted_iota(jnp.int32, (2 * size, size), 1)
            row = jnp.where(row < size, row, row - size)
            live = jnp.logical_and(column < count, row < count)

            def pair(which, carry):
                at = pl.multiple_of(which * 128, 128)
                query = two_heads(qkv[layer, rows, pl.ds(at, 128)], lane_low, lane_high)
                key = qkv[layer, rows, pl.ds(pl.multiple_of(at + width, 128), 128)]
                value = qkv[layer, rows, pl.ds(pl.multiple_of(at + 2 * width, 128), 128)]
                grad = two_heads(mixed_grad[rows, pl.ds(at, 128)], lane_low, lane_high)
                logs = top[layer, rows, pl.ds(at, 128)]
                logs = jnp.concatenate([logs[:, 0:1], logs[:, 64:65]], axis=0)
                probs = jnp.where(live, jnp.exp(dot(query, key, 1, 1) - logs), 0.0)
                d_probs = dot(grad, value, 1, 1)
                centre = jnp.sum(probs * d_probs, axis=-1, keepdims=True)
                d_scores = (probs * (d_probs - centre)).astype(LOW)
                d_query = join_heads(dot(d_scores, key, 1, 0)) * 0.125
                rights[layer, 0, rows, pl.ds(at, 128)] = d_query.astype(LOW)
                rights[layer, 1, rows, pl.ds(at, 128)] = dot(d_scores, query, 0, 0).astype(LOW)
                rights[layer, 2, rows, pl.ds(at, 128)] = dot(probs.astype(LOW), grad, 0, 0).astype(LOW)
                return carry

            lax.fori_loop(0, width // 128, pair, 0)

        plan.each_window(attend)
        fetch(layer, 3).wait()

        def project(size, block, rows):
            grad = state[rows, :]
            for which in range(3):
                columns = slice(which * width, (which + 1) * width)
                piece = rights[layer, which, rows, :]
                grad = grad + dot(piece, wv_qkv[layer, :, columns], 1, 1)
                if which != 1:
                    add_rows(layer, which // 2, piece.astype(F32))
            state[rows, :] = grad
            pltpu.make_async_copy(
                rights.at[layer, :, rows, :], rights_out.at[layer, :, rows, :], out_sem.at[layer, block]
            ).start()

        plan.each_block(project)
        return carry

    lax.fori_loop(0, layers, one_layer, 0)
    for place in range(each):
        hits = marks(row_index, plan.names[place], plan.counts[place], length)
        start = pl.multiple_of(plan.starts[place], 16)
        grad_out[place] = dot(hits, state[pl.ds(start, length), :].astype(LOW), 1, 0).astype(LOW)

    for layer in range(layers):

        def finish(size, block, rows, layer=layer):
            pltpu.make_async_copy(
                rights.at[layer, :, rows, :], rights_out.at[layer, :, rows, :], out_sem.at[layer, block]
            ).wait()

        plan.each_block(finish)


LAGS = (0, 1, 3, 4, 5, 6, 7, 8, 9)
ROUTE = (("var", 1), ("var", 2), ("win", 1), ("win", 2), ("win", 4))


def merge_kernel(
    owners, meta, lefts, rights, sums, layer_out, grad,
    merged, sums_out, layer_back, grad_back,
    left_in, right_in, part, got_core, hold_x, got_x, hold_y, got_y, hold_a, got_a, hold_b, got_b,
    whole, sums_hold, sums_got,
    in_sem, send_sem, recv_sem, out_sem, sums_send, sums_recv, back_send, back_recv, own_sem,
):
    chunks = merged.shape[0]
    layers = lefts.shape[0]
    per_layer = chunks // layers
    packed, width = left_in.shape[1], left_in.shape[2]
    part_rows = part.shape[3]
    each = layer_out.shape[0]
    rows = layer_back.shape[1]
    win, var = lax.axis_index("win"), lax.axis_index("var")
    core, x_half = half_of(var, 1), half_of(var, 2)
    y_half, a_half, b_half = half_of(win, 1), half_of(win, 2), half_of(win, 4)
    others = [flip(var, 1), flip(var, 2), flip(flip(var, 1), 2)]
    route = [partner(axis, bit) for axis, bit in ROUTE]
    greet(route + [(win, others[2])])
    total = meta[meta.shape[0] - 1]

    def block_of(chunk):
        layer, place = layers - 1 - chunk // per_layer, lax.rem(chunk, per_layer)
        group, member = place // 4, lax.rem(place, 4)
        first, third = (2 - group) // 2, group // 2
        second = 1 - first - third
        alone = 1 - (member + 3) // 4
        left = first * (3 + member) + second * 2 + third * alone
        right = first * 8 + second * (4 + member) + third * (member - 1 + 4 * alone)
        return layer, left, right

    def loads(chunk):
        layer, left, right = block_of(chunk)
        slot = lax.rem(chunk, 2)
        return (
            pltpu.make_async_copy(lefts.at[layer, left], left_in.at[slot], in_sem.at[0, slot]),
            pltpu.make_async_copy(rights.at[layer, right], right_in.at[slot], in_sem.at[1, slot]),
        )

    quarter = part_rows // 2
    eighth = quarter // 2
    sixteenth = eighth // 2
    at_y = pl.multiple_of(y_half * quarter, sixteenth)
    at_a = pl.multiple_of(at_y + a_half * eighth, sixteenth)
    at_b = pl.multiple_of(at_a + b_half * sixteenth, sixteenth)

    def exchange(stage, chunk):
        if stage == 0:
            source, target = part.at[chunk, 1 - core], got_core.at[chunk]
        elif stage == 1:
            source, target = hold_x.at[chunk, 1 - x_half], got_x.at[chunk]
        elif stage == 2:
            source, target = hold_y.at[chunk, 1 - y_half], got_y.at[chunk]
        elif stage == 3:
            source, target = hold_a.at[chunk, 1 - a_half], got_a.at[chunk]
        elif stage == 4:
            source, target = hold_b.at[chunk, 1 - b_half], got_b.at[chunk]
        else:
            at, size = ((at_b, sixteenth), (at_a, eighth), (at_y, quarter))[stage - 5]
            source = whole.at[chunk, pl.ds(at, size), :]
            target = source
        return pltpu.make_async_remote_copy(
            src_ref=source,
            dst_ref=target,
            send_sem=send_sem.at[stage, chunk],
            recv_sem=recv_sem.at[stage, chunk],
            device_id=route[(0, 1, 2, 3, 4, 4, 3, 2)[stage]],
            device_id_type=MESH,
        )

    def out_copy(chunk):
        return pltpu.make_async_copy(whole.at[chunk], merged.at[chunk], out_sem.at[chunk])

    def produce(chunk):
        for copy in loads(chunk):
            copy.wait()
        slot = lax.rem(chunk, 2)
        live = lax.broadcasted_iota(jnp.int32, (packed, width), 0) < total
        left = jnp.where(live, left_in[slot], LOW(0))
        right = jnp.where(live, right_in[slot], LOW(0))
        product = dot(left, right, 0, 0).astype(LOW)
        for shard in range(owners):
            part[chunk, shard % 2, shard // 2] = product[shard * part_rows : (shard + 1) * part_rows]
        exchange(0, chunk).start()

    def add(mine, theirs):
        return (mine.astype(F32) + theirs.astype(F32)).astype(LOW)

    def take(stage, chunk):
        exchange(stage - 1, chunk).wait_recv()
        if stage == 1:
            hold_x[chunk] = add(part[chunk, core], got_core[chunk])
        elif stage == 2:
            hold_y[chunk] = add(hold_x[chunk, x_half], got_x[chunk]).reshape(hold_y.shape[1:])
        elif stage == 3:
            hold_a[chunk] = add(hold_y[chunk, y_half], got_y[chunk]).reshape(hold_a.shape[1:])
        elif stage == 4:
            hold_b[chunk] = add(hold_a[chunk, a_half], got_a[chunk]).reshape(hold_b.shape[1:])
        elif stage == 5:
            whole[chunk, pl.ds(at_b, sixteenth), :] = add(hold_b[chunk, b_half], got_b[chunk])
        if stage < 8:
            exchange(stage, chunk).start()
        else:
            out_copy(chunk).start()

    def sums_exchange(turn):
        return pltpu.make_async_remote_copy(
            src_ref=sums_hold.at[turn],
            dst_ref=sums_got.at[turn],
            send_sem=sums_send.at[turn],
            recv_sem=sums_recv.at[turn],
            device_id=route[turn],
            device_id_type=MESH,
        )

    def back_copies():
        sent = []
        for which, (source, target) in enumerate(((grad, grad_back), (layer_out, layer_back))):
            for place, other in enumerate(others):
                sent.append(
                    pltpu.make_async_remote_copy(
                        src_ref=source.at[:, pl.ds(pl.multiple_of(other * rows, rows), rows), :],
                        dst_ref=target.at[pl.ds(var * each, each)],
                        send_sem=back_send.at[which, place],
                        recv_sem=back_recv.at[which, place],
                        device_id=(win, other),
                        device_id_type=MESH,
                    )
                )
        return sent

    def own_copies():
        return [
            pltpu.make_async_copy(
                source.at[:, pl.ds(pl.multiple_of(var * rows, rows), rows), :],
                target.at[pl.ds(var * each, each)],
                own_sem.at[which],
            )
            for which, (source, target) in enumerate(((grad, grad_back), (layer_out, layer_back)))
        ]

    for copy in loads(0):
        copy.start()
    for copy in own_copies():
        copy.start()
    sums_hold[0] = sums[...]
    sums_exchange(0).start()

    def step(now, carry):
        @pl.when(now + 1 < chunks)
        def _():
            for copy in loads(now + 1):
                copy.start()

        @pl.when(now < chunks)
        def _():
            produce(now)

        for stage in range(1, 9):
            lag = LAGS[stage]

            @pl.when(jnp.logical_and(now >= lag, now < chunks + lag))
            def _(stage=stage, lag=lag):
                take(stage, now - lag)

        for turn in range(5):

            @pl.when(now == 2 * turn + 4)
            def _(turn=turn):
                sums_exchange(turn).wait_recv()
                summed = sums_hold[turn] + sums_got[turn]
                if turn < 4:
                    sums_hold[turn + 1] = summed
                    sums_exchange(turn + 1).start()
                else:
                    sums_out[...] = summed

        @pl.when(now == chunks + 1)
        def _():
            for copy in back_copies():
                copy.start()

        return carry

    lax.fori_loop(0, chunks + LAGS[8], step, 0)

    def settle(chunk, carry):
        for stage in range(8):
            exchange(stage, chunk).wait_send()
        out_copy(chunk).wait()
        return carry

    lax.fori_loop(0, chunks, settle, 0)
    for turn in range(5):
        sums_exchange(turn).wait_send()
    for copy in own_copies():
        copy.wait()
    for copy in back_copies():
        copy.wait()


SETTLED = (2, 3, 4, 5, 6, 7, 8)
LAG = 2
DEPTH = 4
Y_FIRST = (1, 7)
Z_FIRST = (4, 10)


class Network:
    def __init__(self, owners, part, got, whole, merged, send_sem, recv_sem, out_sem):
        self.owners, self.part, self.got, self.whole = owners, part, got, whole
        self.merged, self.send_sem, self.recv_sem, self.out_sem = merged, send_sem, recv_sem, out_sem
        self.chunks, self.rows = whole.shape[0], whole.shape[1]
        self.ring = part.shape[0]
        win, var = lax.axis_index("win"), lax.axis_index("var")
        self.win, self.var = win, var
        self.core = half_of(var, 1)
        self.along = {
            "core": (self.core, (win, flip(var, 1))),
            "x": (half_of(var, 2), (win, flip(var, 2))),
            "y": (half_of(win, 1), (flip(win, 1), var)),
            "z": (half_of(win, 2), (flip(win, 2), var)),
            "w": (half_of(win, 4), (flip(win, 4), var)),
        }
        unit, at, self.places = self.rows // 8, 0, {}
        for stage, name in ((7, "y"), (6, "z"), (5, "w")):
            size = (1 << (stage - 5)) * unit
            at = pl.multiple_of(at + self.along[name][0] * size, size)
            self.places[stage] = (at, size)

    @staticmethod
    def way(chunk):
        place = chunk % 12

        def among(chosen):
            return sum(1 - ((place - one) * (place - one) + 143) // 144 for one in chosen)

        return among(Y_FIRST), among(Z_FIRST)

    def hop(self, stage, chunk):
        name = ("core", "x", "y", "z", "w", "w", "z", "y")[stage]
        if stage not in (1, 2, 3):
            return self.along[name]
        y_first, z_first = self.way(chunk)
        shares = {
            1: ((1 - y_first - z_first, "x"), (y_first, "y"), (z_first, "z")),
            2: ((1 - y_first - z_first, "y"), (y_first + z_first, "x")),
            3: ((1 - z_first, "z"), (z_first, "y")),
        }[stage]
        half, win, var = 0, 0, 0
        for share, name in shares:
            bit, (to_win, to_var) = self.along[name]
            half, win, var = half + share * bit, win + share * to_win, var + share * to_var
        return half, (win, var)

    def part_of(self, stage, half):
        size = self.got[stage].shape[1]
        return pl.ds(pl.multiple_of(half * size, 16), size)

    def exchange(self, stage, chunk):
        half, beyond = self.hop(stage, chunk)
        if stage == 0:
            source, target = self.part.at[chunk % self.ring, 1 - half], self.got[0].at[chunk]
        elif stage < 5:
            source, target = self.got[stage - 1].at[chunk, self.part_of(stage, 1 - half), :], self.got[stage].at[chunk]
        else:
            at, size = self.places[stage]
            source = target = self.whole.at[chunk, pl.ds(at, size), :]
        return pltpu.make_async_remote_copy(
            src_ref=source,
            dst_ref=target,
            send_sem=self.send_sem.at[stage, chunk],
            recv_sem=self.recv_sem.at[stage, chunk],
            device_id=beyond,
            device_id_type=MESH,
        )

    def out_copy(self, chunk):
        return pltpu.make_async_copy(self.whole.at[chunk], self.merged.at[chunk], self.out_sem.at[chunk])

    def emit(self, chunk, place, left, right):
        product = dot(left, right, 0, 0).astype(LOW)
        slot = chunk % self.ring

        @pl.when(chunk >= self.ring)
        def _():
            self.exchange(0, chunk - self.ring).wait_send()

        rows, quarter = self.rows, self.rows // 4
        y_first, z_first = self.way(place)
        for shard in range(self.owners):
            core, x = shard % 2, shard // 2
            for y in range(2):
                for z in range(2):
                    straight, over_y, over_z = 4 * x + 2 * y + z, 4 * y + 2 * x + z, 4 * z + 2 * x + y
                    at = straight + y_first * (over_y - straight) + z_first * (over_z - straight)
                    here = shard * rows + (2 * y + z) * quarter
                    self.part[slot, core, pl.ds(at * quarter, quarter), :] = product[here : here + quarter]
        self.exchange(0, chunk).start()

    def take(self, stage, chunk):
        def add(mine, target):
            return (mine.astype(F32) + target[chunk].astype(F32)).astype(LOW)

        self.exchange(stage - 1, chunk).wait_recv()
        if stage == 1:
            target = self.got[0]
            target[chunk] = add(self.part[chunk % self.ring, self.core], target)
        elif stage <= 4:
            half, _ = self.hop(stage - 1, chunk)
            target = self.got[stage - 1]
            target[chunk] = add(self.got[stage - 2][chunk, self.part_of(stage - 1, half), :], target)
        elif stage == 5:
            half, _ = self.hop(4, chunk)
            at, unit = self.places[5]
            self.whole[chunk, pl.ds(at, unit), :] = add(self.got[3][chunk, self.part_of(4, half), :], self.got[4])
        if stage == 1:

            @pl.when(chunk < DEPTH)
            def _():
                self.exchange(1, chunk).start()
        elif stage < 8:
            self.exchange(stage, chunk).start()
        else:
            self.out_copy(chunk).start()

    def pump(self, turn):
        for place, stage in enumerate(SETTLED):
            chunk = turn - LAG * place

            @pl.when(jnp.logical_and(chunk >= 0, chunk < self.chunks))
            def _(stage=stage, chunk=chunk):
                self.take(stage, chunk)

            if place == 0:

                @pl.when(turn + DEPTH < self.chunks)
                def _():
                    self.exchange(1, turn + DEPTH).start()

    def settle(self):
        def one(chunk, carry):
            for stage in range(1, 8):
                self.exchange(stage, chunk).wait_send()
            self.out_copy(chunk).wait()
            return carry

        lax.fori_loop(0, self.chunks, one, 0)
        for chunk in range(self.chunks - self.ring, self.chunks):
            self.exchange(0, chunk).wait_send()


def packed_kernel(
    owners, size,
    windows, row_index, inputs, cotangent, w_qkv, w_attn, w_in, w_out, bias_qv, out_bias, bias_in, gain, shift,
    merged, sums_out, layer_back, grad_back, meta,
    x_stage, x, most, most_got, wv_qkv, wv_attn, wv_in, wv_out, g_stage, g, spots, state, lefts, rights, qkv, slope,
    normal, inverse, top, mixed_grad, last_right, sums, part, got_core, got_one, got_two, got_three, got_four, whole,
    sums_hold, sums_got,
    weight_sem, send_sem, recv_sem, out_sem, sums_send, sums_recv, far_send, far_recv, own_sem, most_send, most_recv,
):
    each, length, width = x.shape
    wins, rows = cotangent.shape[0], cotangent.shape[1]
    layers = w_qkv.shape[0]
    hidden_width = w_in.shape[2]
    pieces = hidden_width // width
    strip = width // pieces
    pairs = width // 128
    got = (got_core, got_one, got_two, got_three, got_four)
    layer_out, grad_out = x, g
    net = Network(owners, part, got, whole, merged, send_sem, recv_sem, out_sem)
    win, var = net.win, net.var
    others = [flip(var, 1), flip(var, 2), flip(flip(var, 1), 2)]
    weights = ((w_qkv, wv_qkv), (w_attn, wv_attn), (w_in, wv_in), (w_out, wv_out))

    def fetch(layer, which):
        source, target = weights[which]
        return pltpu.make_async_copy(source.at[layer], target.at[layer], weight_sem.at[layer, which])

    for layer in range(layers):
        for which in range(4):
            fetch(layer, which).start()

    barrier = pltpu.get_barrier_semaphore()
    across = [(flip(win, bit), var) for bit in (1, 2, 4)]
    friends = [(win, other) for other in others] + across
    for friend in friends:
        pl.semaphore_signal(barrier, inc=1, device_id=friend, device_id_type=MESH)
    order = assign(windows, wins, owners)
    for place in range(wins):
        meta[place] = order[place]
        x_stage[place] = inputs[order[place]]
    meta[wins] = var
    pl.semaphore_wait(barrier, len(friends))
    mine = pl.ds(pl.multiple_of(var * rows, rows), rows)

    def remote(source, target, which, place, other):
        return pltpu.make_async_remote_copy(
            src_ref=source,
            dst_ref=target,
            send_sem=far_send.at[which, place],
            recv_sem=far_recv.at[which, place],
            device_id=(win, other),
            device_id_type=MESH,
        )

    def to_owners(stage, target, which):
        return [
            remote(stage.at[pl.ds(other * each, each)], target.at[:, mine, :], which, place, other)
            for place, other in enumerate(others)
        ] + [pltpu.make_async_copy(stage.at[pl.ds(var * each, each)], target.at[:, mine, :], own_sem.at[which])]

    def to_slots(source, target, which):
        home = target.at[pl.ds(var * each, each)]
        return [
            remote(source.at[:, pl.ds(pl.multiple_of(other * rows, rows), rows), :], home, which, place, other)
            for place, other in enumerate(others)
        ] + [pltpu.make_async_copy(source.at[:, mine, :], home, own_sem.at[which])]

    for copy in to_owners(x_stage, x, 3):
        copy.start()
    for place in range(wins):
        g_stage[place] = cotangent[order[place]]

    names, counts = [], []
    for place in range(each):
        name = order[place]
        for owner in range(1, owners):
            name = jnp.where(var == owner, order[owner * each + place], name)
        names.append(name)
        counts.append(windows[name])

    starts = [jnp.int32(0)]
    for count in counts:
        starts.append(starts[-1] + count)
    for place in range(each):
        hits = marks(row_index, names[place], counts[place], length)
        along = lax.broadcasted_iota(jnp.int32, (length, size), 0) + starts[place]
        moved = jnp.where(lax.broadcasted_iota(jnp.int32, (length, size), 1) == along, 1.0, 0.0).astype(LOW)
        spots[place * length : (place + 1) * length] = dot(hits, moved, 1, 0).astype(LOW)

    row = lax.broadcasted_iota(jnp.int32, (size, 128), 0)
    lane = lax.broadcasted_iota(jnp.int32, (size, 128), 1)
    owner = jnp.zeros((size, 128), jnp.int32)
    for start in starts[1:]:
        owner = owner + jnp.where(row >= start, 1, 0)
    key_mark = jnp.where(lane == owner, 1.0, 0.0).astype(LOW)
    query_mark = jnp.where(lane == owner, jnp.where(lane < each, 0.0, -1e30), -1e30).astype(LOW)
    query_mark = jnp.concatenate([query_mark, query_mark], axis=0)
    lane_low, lane_high = lane_masks(128)

    largest = jnp.int32(0)
    for owner in range(owners):
        total = jnp.int32(0)
        for place in range(each):
            total = total + windows[order[owner * each + place]]
        largest = jnp.maximum(largest, total)
    most[0] = jnp.full(most.shape[1:], largest, jnp.int32)
    for turn, friend in enumerate(across):
        copy = pltpu.make_async_remote_copy(
            src_ref=most.at[turn],
            dst_ref=most_got.at[turn],
            send_sem=most_send.at[turn],
            recv_sem=most_recv.at[turn],
            device_id=friend,
            device_id_type=MESH,
        )
        copy.start()
        copy.wait()
        most[turn + 1] = jnp.maximum(most[turn], most_got[turn])
    meta[wins + 1] = jnp.max(most[len(across)])
    for copy in to_owners(x_stage, x, 3):
        copy.wait()
    for copy in to_owners(g_stage, g, 0):
        copy.start()
    state[...] = dot(spots[...], x[...].reshape(each * length, width), 0, 0)
    fetch(0, 0).wait()

    def masked_scores(layer, at):
        query = two_heads(qkv[layer, :, pl.ds(at, 128)], lane_low, lane_high)
        key = qkv[layer, :, pl.ds(at + width, 128)]
        value = qkv[layer, :, pl.ds(at + 2 * width, 128)]
        scores = dot(
            jnp.concatenate([key, key_mark], axis=1), jnp.concatenate([query, query_mark], axis=1), 1, 1
        )
        return query, key, value, scores

    def forward_layer(layer, carry):
        @pl.when(layer > 0)
        def _():
            fetch(layer, 0).wait()

        tokens = state[...].astype(LOW)
        lefts[layer, 0] = tokens
        for which in range(3):
            columns = slice(which * width, (which + 1) * width)
            joint = dot(tokens, wv_qkv[layer, :, columns], 1, 0)
            if which == 0:
                joint = (joint + bias_qv[pl.ds(layer, 1), :width]).astype(LOW) * LOW(0.125)
            elif which == 2:
                joint = (joint + bias_qv[pl.ds(layer, 1), width:]).astype(LOW)
            else:
                joint = joint.astype(LOW)
            qkv[layer, :, columns] = joint
        for pair in range(pairs):
            at = pair * 128
            _, _, value, scores = masked_scores(layer, at)
            peak = jnp.max(scores, axis=0, keepdims=True)
            expo = jnp.exp(scores - peak)
            total = jnp.sum(expo, axis=0, keepdims=True)
            probs = (expo * (1.0 / total)).astype(LOW)
            lefts[layer, 1, :, pl.ds(at, 128)] = join_heads(dot(probs, value, 0, 0)).astype(LOW)
            top[layer, pair] = peak + jnp.log(total)
        for which in range(1, 4):
            fetch(layer, which).wait()
        first = dot(lefts[layer, 1], wv_attn[layer], 1, 0) + out_bias[layer, 0:1, :]
        one, inverse_one = normalize(state[...] + first)
        normal[layer, 0] = one
        after = one * gain[layer, 0:1, :] + shift[layer, 0:1, :]
        after_low = after.astype(LOW)
        lefts[layer, 2] = after_low
        second = jnp.zeros((size, width), F32)
        for piece in range(pieces):
            columns = slice(piece * width, (piece + 1) * width)
            hidden = dot(after_low, wv_in[layer, :, columns], 1, 0) + bias_in[pl.ds(layer, 1), columns]
            squared = hidden * hidden
            bend = jnp.tanh(hidden * (SMOOTH + SMOOTH * CUBIC * squared))
            half = 0.5 + 0.5 * bend
            active = (hidden * half).astype(LOW)
            rise = half + (hidden * half) * (1.0 - bend) * (SMOOTH + SMOOTH * 3.0 * CUBIC * squared)
            slope[layer, :, columns] = rise.astype(LOW)
            for sub in range(pieces):
                lefts[layer, 3 + sub, :, piece * strip : (piece + 1) * strip] = active[
                    :, sub * strip : (sub + 1) * strip
                ]
            second = second + dot(active, wv_out[layer, columns, :], 1, 0)
        two, inverse_two = normalize(after + second + out_bias[layer, 1:2, :])
        normal[layer, 1] = two
        state[...] = two * gain[layer, 1:2, :] + shift[layer, 1:2, :]
        lanes = lax.broadcasted_iota(jnp.int32, (size, 128), 1)
        inverse[layer] = jnp.where(lanes < 64, inverse_one, inverse_two)
        return carry

    lax.fori_loop(0, layers, forward_layer, 0)
    layer_out[...] = dot(spots[...], state[...].astype(LOW), 1, 0).astype(LOW).reshape(layer_out.shape)
    for copy in to_owners(g_stage, g, 0):
        copy.wait()
    state[...] = dot(spots[...], g[...].reshape(each * length, width), 0, 0)
    sums[...] = jnp.zeros_like(sums)

    def add_rows(layer, place, values):
        sums[layer, place : place + 1, :] += jnp.sum(values, axis=0, keepdims=True)

    per_layer = net.chunks // layers

    def backward_layer(step, carry):
        layer = layers - 1 - step
        first = step * per_layer
        turn = step * 7

        def emit(place, left, right):
            net.emit(first + place, place, left, right)

        def take(place):
            net.take(1, first + place)

        grad = state[...]
        two = normal[layer, 1]
        back = normalize_back(grad, gain[layer, 1:2, :], two, inverse[layer, :, 64:65])
        back_low = back.astype(LOW)
        last_right[...] = back_low

        def outer(piece, carry):
            emit(piece, lefts[layer, 3 + piece], last_right[...])

            @pl.when(piece > 0)
            def _():
                take(piece - 1)

            return carry

        lax.fori_loop(0, pieces, outer, 0)
        add_rows(layer, 9, grad * two)
        add_rows(layer, 11, grad)
        add_rows(layer, 3, back_low.astype(F32))
        state[...] = back

        def inner(piece, carry):
            columns = pl.ds(pl.multiple_of(piece * width, width), width)
            active = dot(last_right[...], wv_out[layer, columns, :], 1, 1)
            hidden = (active * slope[layer, :, columns].astype(F32)).astype(LOW)
            sums[layer, pl.ds(4 + piece, 1), :] = jnp.sum(hidden.astype(F32), axis=0, keepdims=True)
            rights[0] = hidden
            emit(pieces + piece, lefts[layer, 2], rights[0])
            state[...] += dot(rights[0], wv_in[layer, :, columns], 1, 1)
            take(pieces + piece - 1)

            @pl.when(piece > 0)
            def _():
                net.pump(turn + piece - 1)

            return carry

        lax.fori_loop(0, pieces, inner, 0)
        back = state[...]
        one = normal[layer, 0]
        add_rows(layer, 8, back * one)
        add_rows(layer, 10, back)
        back = normalize_back(back, gain[layer, 0:1, :], one, inverse[layer, :, 0:1])
        back_low = back.astype(LOW)
        emit(8, lefts[layer, 1], back_low)
        take(7)
        add_rows(layer, 2, back_low.astype(F32))
        mixed_grad[...] = dot(back_low, wv_attn[layer], 1, 1).astype(LOW)
        state[...] = back
        net.pump(turn + 3)
        for pair in range(pairs):
            at = pair * 128
            query, key, value, scores = masked_scores(layer, at)
            grads = two_heads(mixed_grad[:, pl.ds(at, 128)], lane_low, lane_high)
            probs = jnp.exp(scores - top[layer, pair])
            d_probs = dot(value, grads, 1, 1)
            centre = jnp.sum(probs * d_probs, axis=0, keepdims=True)
            d_scores = (probs * (d_probs - centre)).astype(LOW)
            d_query = join_heads(dot(d_scores, key, 0, 0)) * 0.125
            rights[0, :, pl.ds(at, 128)] = d_query.astype(LOW)
            rights[1, :, pl.ds(at, 128)] = dot(d_scores, query, 1, 0).astype(LOW)
            rights[2, :, pl.ds(at, 128)] = dot(probs.astype(LOW), grads, 1, 0).astype(LOW)
        take(8)
        net.pump(turn + 4)

        def last(which, carry):
            emit(9 + which, lefts[layer, 0], rights[which])

            @pl.when(which > 0)
            def _():
                take(8 + which)

            return carry

        lax.fori_loop(0, 3, last, 0)
        net.pump(turn + 5)
        grad = state[...]
        for which in range(3):
            piece = rights[which]
            grad = grad + dot(piece, wv_qkv[layer, :, which * width : (which + 1) * width], 1, 1)
            if which != 1:
                add_rows(layer, which // 2, piece.astype(F32))
        state[...] = grad
        take(11)
        net.pump(turn + 6)
        return carry

    lax.fori_loop(0, layers, backward_layer, 0)
    first_turn = 7 * layers
    grad_out[...] = dot(spots[...], state[...].astype(LOW), 1, 0).astype(LOW).reshape(grad_out.shape)

    route = [partner(axis, bit) for axis, bit in ROUTE]

    def sums_exchange(step):
        return pltpu.make_async_remote_copy(
            src_ref=sums_hold.at[step],
            dst_ref=sums_got.at[step],
            send_sem=sums_send.at[step],
            recv_sem=sums_recv.at[step],
            device_id=route[step],
            device_id_type=MESH,
        )

    sums_hold[0] = sums[...]
    sums_exchange(0).start()

    def step(now, carry):
        net.pump(now)

        @pl.when(now == net.chunks - 1)
        def _():
            for copy in to_slots(grad_out, grad_back, 2) + to_slots(layer_out, layer_back, 1):
                copy.start()

        for place in range(5):

            @pl.when(now == first_turn + 1 + 2 * place)
            def _(place=place):
                sums_exchange(place).wait_recv()
                summed = sums_hold[place] + sums_got[place]
                if place < 4:
                    sums_hold[place + 1] = summed
                    sums_exchange(place + 1).start()
                else:
                    sums_out[...] = summed

        return carry

    lax.fori_loop(first_turn, net.chunks + LAG * (len(SETTLED) - 1), step, 0)
    net.settle()
    for place in range(5):
        sums_exchange(place).wait_send()
    for copy in to_slots(layer_out, layer_back, 1) + to_slots(grad_out, grad_back, 2):
        copy.wait()


def finish_kernel(
    at_var, meta, sums, merged, layer_back, grad_back,
    layer_out, grad_inputs, qkv, attn, in_, out, bias_qv, out_bias, bias_in, gain, shift,
    chunks, layer_in, grad_in, grad_wide, qkv_wide, attn_wide, in_wide, out_wide, in_sem, out_sem,
):
    wins, rows = layer_back.shape[0], layer_back.shape[1]
    layers, width = qkv.shape[0], merged.shape[2]
    part_rows = merged.shape[1]
    per_layer = merged.shape[0] // layers
    loads = [
        pltpu.make_async_copy(grad_back, grad_in, in_sem.at[0]),
        pltpu.make_async_copy(layer_back, layer_in, in_sem.at[1]),
    ] + [
        pltpu.make_async_copy(
            merged.at[pl.ds(half * per_layer, per_layer)], chunks.at[pl.ds(half * per_layer, per_layer)], in_sem.at[2 + half]
        )
        for half in range(layers)
    ]
    for load in loads:
        load.start()

    def home(place):
        window = meta[place]
        return (
            pltpu.make_async_copy(grad_wide.at[place], grad_inputs.at[window], out_sem.at[0, place]),
            pltpu.make_async_copy(layer_in.at[place], layer_out.at[window], out_sem.at[1, place]),
        )

    def outs(layer):
        return [
            pltpu.make_async_copy(source.at[layer], target.at[layer], out_sem.at[2 + layer, which])
            for which, (source, target) in enumerate(
                ((qkv_wide, qkv), (attn_wide, attn), (in_wide, in_), (out_wide, out))
            )
        ]

    loads[0].wait()
    loads[1].wait()

    def send(place, carry):
        grad_wide[place] = grad_in[place].astype(F32)
        for copy in home(place):
            copy.start()
        return carry

    lax.fori_loop(0, wins, send, 0)
    for half in range(layers):
        loads[2 + half].wait()
        layer, base = layers - 1 - half, half * per_layer

        def widen(block, carry, layer=layer, base=base):
            at = pl.multiple_of(block * 32, 32)
            here = pl.ds(at, 32)
            for which in range(4):
                columns = slice(which * width, (which + 1) * width)
                there = pl.ds(pl.multiple_of(at + which * part_rows, 32), 32)
                out_wide[layer, there, :] = chunks[base + which, here, :].astype(F32)
                in_wide[layer, here, columns] = chunks[base + 4 + which, here, :].astype(F32)
                if which < 3:
                    qkv_wide[layer, here, columns] = chunks[base + 9 + which, here, :].astype(F32)
            attn_wide[layer, here, :] = chunks[base + 8, here, :].astype(F32)
            return carry

        lax.fori_loop(0, part_rows // 32, widen, 0)
        for copy in outs(layer):
            copy.start()

    var = meta[at_var]
    narrow = out_bias.shape[2]
    at = pl.multiple_of(var * narrow, narrow)
    wide = bias_qv.shape[1]
    for layer in range(layers):
        half = width // wide
        bias_qv[layer : layer + 1, :] = sums[
            layer, pl.ds(var // half, 1), pl.ds(pl.multiple_of(lax.rem(var, half) * wide, wide), wide)
        ]
        bias_in[layer : layer + 1, :] = sums[layer, pl.ds(4 + var, 1), :]
        out_bias[layer] = sums[layer, 2:4, pl.ds(at, narrow)]
        gain[layer] = sums[layer, 8:10, pl.ds(at, narrow)]
        shift[layer] = sums[layer, 10:12, pl.ds(at, narrow)]

    def settle(place, carry):
        for copy in home(place):
            copy.wait()
        return carry

    lax.fori_loop(0, wins, settle, 0)
    for layer in range(layers):
        for copy in outs(layer):
            copy.wait()


def gather_kernel(owners, meta, x, x_out, x_stage, x_send, x_recv, own_sem):
    wins, rows = x.shape[0], x.shape[1]
    each = wins // owners
    me, win = lax.axis_index("var"), lax.axis_index("win")
    others = [(win, flip(me, 1)), (win, flip(me, 2)), (win, flip(flip(me, 1), 2))]
    for place in range(wins):
        x_stage[place] = x[meta[place]]
    greet(others)
    own = pl.ds(pl.multiple_of(me * rows, rows), rows)
    copies = [pltpu.make_async_copy(x_stage.at[pl.ds(me * each, each)], x_out.at[:, own, :], own_sem)]
    for place, other in enumerate(others):
        copies.append(
            pltpu.make_async_remote_copy(
                src_ref=x_stage.at[pl.ds(other[1] * each, each)],
                dst_ref=x_out.at[:, own, :],
                send_sem=x_send.at[place],
                recv_sem=x_recv.at[place],
                device_id=other,
                device_id_type=MESH,
            )
        )
    for copy in copies:
        copy.start()
    for copy in copies:
        copy.wait()


def in_vmem(count):
    return [pl.BlockSpec(memory_space=pltpu.VMEM)] * count


def anywhere(count):
    return [pl.BlockSpec(memory_space=pl.ANY)] * count


def in_smem():
    return [pl.BlockSpec(memory_space=pltpu.SMEM)]


def shaped(shape, kind=LOW):
    return jax.ShapeDtypeStruct(shape, kind)


def whole_windows(
    inputs, counts, row_index, w_qkv, bias_qv, w_attn_out, out_bias, w_in, bias_in, w_ffn_out,
    norm_gain, norm_bias, cotangent,
):
    wins, rows, width = inputs.shape
    owners, groups = lax.axis_size("var"), lax.axis_size("win")
    each, length = wins // owners, rows * owners
    packed = each * length
    layers, hidden_width = w_in.shape[0], w_in.shape[2]
    dma = pltpu.SemaphoreType.DMA

    def params(**more):
        return pltpu.CompilerParams(vmem_limit_bytes=VMEM_BYTES, **more)

    weights = (w_qkv, w_attn_out, w_in, w_ffn_out)
    weight_space = [pltpu.VMEM(weight.shape, LOW) for weight in weights]
    narrow = width // owners
    chunks = layers * 12
    part_rows = width // owners
    half, quarter, eighth = part_rows // 2, part_rows // 4, part_rows // 8
    sums_shape = (layers, 16, width)

    def space(*shape):
        return pltpu.VMEM((chunks,) + shape + (width,), LOW)

    def finish(at_var, meta, merged, sums, layer_back, grad_back):
        rows_shape = (wins, rows, width)
        large = [
            shaped((layers, narrow, 3 * width), F32),
            shaped((layers, narrow, width), F32),
            shaped((layers, narrow, hidden_width), F32),
            shaped((layers, hidden_width // owners, width), F32),
        ]
        layer_out, grad_inputs, *rest = pl.pallas_call(
            functools.partial(finish_kernel, at_var),
            name="finish",
            out_shape=[shaped(rows_shape), shaped(rows_shape, F32)]
            + large
            + [
                shaped((layers, 2 * narrow), F32),
                shaped((layers, 2, narrow), F32),
                shaped((layers, hidden_width // owners), F32),
                shaped((layers, 2, narrow), F32),
                shaped((layers, 2, narrow), F32),
            ],
            in_specs=in_smem() + in_vmem(1) + anywhere(3),
            out_specs=anywhere(6) + in_vmem(5),
            scratch_shapes=[pltpu.VMEM(merged.shape, LOW)]
            + [pltpu.VMEM(rows_shape, LOW)] * 2
            + [pltpu.VMEM(rows_shape, F32)]
            + [pltpu.VMEM(entry.shape, F32) for entry in large]
            + [dma((2 + layers,)), dma((2 + layers, wins))],
            compiler_params=params(),
        )(meta, sums, merged, layer_back, grad_back)
        qkv, attn, in_, out, qv, biases, hidden, gain, shift = rest
        return layer_out, grad_inputs, qkv, qv, attn, biases, in_, hidden, out, gain, shift

    def packed_way():
        size = PACKED
        return pl.pallas_call(
            functools.partial(packed_kernel, owners, size),
            name="packed",
            out_shape=[
                shaped((chunks, part_rows, width)),
                shaped(sums_shape, F32),
                shaped((wins, rows, width)),
                shaped((wins, rows, width)),
                shaped((wins + 2,), jnp.int32),
            ],
            in_specs=in_smem() + in_vmem(3) + anywhere(4) + in_vmem(5),
            out_specs=anywhere(1) + in_vmem(1) + anywhere(2) + in_smem(),
            scratch_shapes=[
                pltpu.VMEM((wins, rows, width), LOW),
                pltpu.VMEM((each, length, width), LOW),
                pltpu.VMEM((4, 8, 128), jnp.int32),
                pltpu.VMEM((3, 8, 128), jnp.int32),
            ]
            + weight_space
            + [
                pltpu.VMEM((wins, rows, width), LOW),
                pltpu.VMEM((each, length, width), LOW),
                pltpu.VMEM((each * length, size), LOW),
                pltpu.VMEM((size, width), F32),
                pltpu.VMEM((layers, 7, size, width), LOW),
                pltpu.VMEM((3, size, width), LOW),
                pltpu.VMEM((layers, size, 3 * width), LOW),
                pltpu.VMEM((layers, size, hidden_width), LOW),
                pltpu.VMEM((layers, 2, size, width), F32),
                pltpu.VMEM((layers, size, 128), F32),
                pltpu.VMEM((layers, width // 128, 1, 2 * size), F32),
                pltpu.VMEM((size, width), LOW),
                pltpu.VMEM((size, width), LOW),
                pltpu.VMEM(sums_shape, F32),
                pltpu.VMEM((4, 2, 2 * part_rows, width), LOW),
                space(2 * part_rows),
                space(part_rows),
                space(half),
                space(quarter),
                space(eighth),
                space(part_rows),
            ]
            + [pltpu.VMEM((5,) + sums_shape, F32)] * 2
            + [dma((layers, 4)), dma((8, chunks)), dma((8, chunks)), dma((chunks,))]
            + [dma((5,))] * 2
            + [dma((4, owners - 1))] * 2
            + [dma((4,))]
            + [dma((3,))] * 2,
            compiler_params=params(collective_id=2, has_side_effects=True),
        )(
            counts, row_index, inputs, cotangent, *weights, bias_qv, out_bias, bias_in, norm_gain, norm_bias
        )

    def ragged_way():
        x, meta = pl.pallas_call(
            functools.partial(spread_kernel, owners),
            name="spread",
            out_shape=[shaped((each, length, width)), shaped((wins + 2 * each + 2,), jnp.int32)],
            in_specs=in_smem() + in_vmem(1),
            out_specs=anywhere(1) + in_smem(),
            scratch_shapes=[
                pltpu.VMEM((wins, rows, width), LOW),
            ]
            + [dma((owners - 1,))] * 2
            + [dma],
            compiler_params=params(collective_id=0, has_side_effects=True),
        )(counts, inputs)
        g = pl.pallas_call(
            functools.partial(gather_kernel, owners),
            name="gather",
            out_shape=shaped((each, length, width)),
            in_specs=in_smem() + in_vmem(1),
            out_specs=pl.BlockSpec(memory_space=pl.ANY),
            scratch_shapes=[pltpu.VMEM((wins, rows, width), LOW)] + [dma((owners - 1,))] * 2 + [dma],
            compiler_params=params(collective_id=3, has_side_effects=True),
        )(meta, cotangent)
        kept = [
            shaped((layers, packed, 3 * width)),
            shaped((layers, packed, hidden_width)),
            shaped((layers, 2, packed, width), F32),
            shaped((layers, packed, 128), F32),
            shaped((layers, packed, width), F32),
        ]
        kept_space = [pltpu.VMEM(entry.shape, entry.dtype) for entry in kept]
        lefts_shape = shaped((layers, 7, packed, width))
        lefts, *stash, layer_rows = pl.pallas_call(
            forward_kernel,
            name="forward",
            out_shape=[lefts_shape] + kept + [shaped((each, length, width))],
            in_specs=in_smem() + in_vmem(2) + anywhere(4) + in_vmem(5),
            out_specs=anywhere(6) + in_vmem(1),
            scratch_shapes=weight_space
            + [pltpu.VMEM(lefts_shape.shape, LOW)]
            + kept_space
            + [pltpu.VMEM((packed, width), F32), dma((layers, 4)), dma((layers, 6, 6))],
            compiler_params=params(),
        )(meta, row_index, x, *weights, bias_qv, out_bias, bias_in, norm_gain, norm_bias)

        rights_shape = shaped((layers, 9, packed, width))
        rights, grad_rows, sums = pl.pallas_call(
            backward_kernel,
            name="backward",
            out_shape=[rights_shape, shaped((each, length, width)), shaped((layers, 16, width), F32)],
            in_specs=in_smem() + in_vmem(2) + anywhere(4) + in_vmem(1) + anywhere(5),
            out_specs=anywhere(1) + in_vmem(2),
            scratch_shapes=weight_space
            + [pltpu.VMEM(rights_shape.shape, LOW)]
            + kept_space
            + [
                pltpu.VMEM((packed, width), F32),
                pltpu.VMEM((packed, width), LOW),
                dma((layers, 4)),
                dma((layers, 5, 6)),
                dma((layers, 6)),
            ],
            compiler_params=params(),
        )(meta, row_index, g, *weights, norm_gain, *stash)

        merged, sums, layer_back, grad_back = pl.pallas_call(
            functools.partial(merge_kernel, owners),
            name="merge",
            out_shape=[
                shaped((chunks, part_rows, width)),
                shaped(sums.shape, F32),
                shaped((wins, rows, width)),
                shaped((wins, rows, width)),
            ],
            in_specs=in_smem() + anywhere(2) + in_vmem(3),
            out_specs=anywhere(1) + in_vmem(1) + anywhere(2),
            scratch_shapes=[pltpu.VMEM((2, packed, width), LOW)] * 2
            + [
                space(2, 2, part_rows),
                space(2, part_rows),
                space(2, part_rows),
                space(part_rows),
                space(2, half),
                space(half),
                space(2, quarter),
                space(quarter),
                space(2, eighth),
                space(eighth),
                space(part_rows),
            ]
            + [pltpu.VMEM((5,) + sums.shape, F32)] * 2
            + [dma((2, 2)), dma((8, chunks)), dma((8, chunks)), dma((chunks,))]
            + [dma((5,))] * 2
            + [dma((2, owners - 1))] * 2
            + [dma((2,))],
            compiler_params=params(collective_id=1, has_side_effects=True),
        )(meta, lefts, rights, sums, layer_rows, grad_rows)
        return finish(wins + 2 * each, meta, merged, sums, layer_back, grad_back)

    *sums_up, order = packed_way()
    return lax.cond(order[wins + 1] <= PACKED, lambda: finish(wins, order, *sums_up), ragged_way)


def choose(*arrays):
    wins, rows, width = arrays[0].shape
    owners, groups = lax.axis_size("var"), lax.axis_size("win")
    fits = owners == 4 and groups == 8 and wins % owners == 0 and rows % 16 == 0
    fits = fits and (wins // owners, rows * owners, width, arrays[7].shape[2]) == (3, 256, 512, 2048)
    return whole_windows(*arrays) if fits else per_device(*arrays)


def solution(mesh):
    return jax.shard_map(
        choose,
        mesh=mesh,
        in_specs=(
            P("win", "var", None),
            P("win"),
            P("win", None),
            P(),
            P(),
            P(),
            P(),
            P(),
            P(),
            P(),
            P(),
            P(),
            P("win", "var", None),
        ),
        out_specs=(
            P("win", "var", None),
            P("win", "var", None),
            P(None, "var", None),
            P(None, "var"),
            P(None, "var", None),
            P(None, None, "var"),
            P(None, "var", None),
            P(None, "var"),
            P(None, "var", None),
            P(None, None, "var"),
            P(None, None, "var"),
        ),
        check_vma=False,
    )
```

profile of v0, /device:TPU:0, one launch (start us, length us, event | category | flops | bytes accessed | tf_op | source)
XLA Modules:
  0.0 147.7 jit_solution(6059361839950758984)
XLA Ops:
  0.6 0.0 copy-start
  0.7 0.0 copy-start.1
  0.7 0.0 copy-start.2
  0.7 0.0 copy-start.3
  0.7 0.0 copy-start.4
  0.7 0.0 copy-start.5
  0.7 0.0 copy-start.6
  0.7 0.0 copy-start.7
  0.7 0.0 copy-start.8
  0.7 139.0 %packed.1 = (bf16[24,128,512]{2,1,0:T(8,128)(2,1)}, f32[2,16,512]{2,1,0:T(8,128)S(1)}, bf16[12,64,512]{2,1,0:T(8,128)(2,1)}, bf16[12,64,512]{2,1,0:T(8,128)(2,1)}, s32[14]{0:T(128)S(1)}) custom-call(s32[12]{0:T(128)} %windows.1, s32[12,256]{1,0:T(8,128)} %row_index.1, bf16[12,64,512]{2,1,0:T(8,128)(2,1)} %inputs.1, bf16[12,64,512]{2,1,0:T(8,128)(2,1)} %cotangent.1, ...), custom_call_target="tpu_custom_call" | custom-call | tf_op jit(solution)/shard_map/packed/pallas_call | solution.py:1690
  139.8 0.6 slice.3
  141.0 0.0 copy-done
  141.0 0.0 copy-done.1
  141.0 0.0 copy-done.2
  141.0 0.0 copy-done.3
  141.0 0.0 copy-done.4
  141.1 0.0 copy-done.5
  141.1 0.0 copy-done.6
  141.1 0.0 copy-done.7
  141.1 0.0 copy-done.8
  141.1 6.4 %conditional.1 = (bf16[12,64,512]{2,1,0:T(8,128)(2,1)}, f32[12,64,512]{2,1,0:T(8,128)}, f32[2,128,1536]{2,1,0:T(8,128)}, f32[2,256]{1,0:T(2,128)}, f32[2,128,512...) conditional(s32[]{:T(128)} %bitcast, (s32[12]{0:T(128)S(1)}, ...), branch_computations={%region_0.0_spmd, %region_1.0_spmd} | conditional | bytes 88 | solution.py:1843
  141.1 6.4 %finish.3 = (bf16[12,64,512]{2,1,0:T(8,128)(2,1)}, f32[12,64,512]{2,1,0:T(8,128)}, f32[2,128,1536]{2,1,0:T(8,128)}, f32[2,128,512]{2,1,0:T(8,128)}, f32[2,128,20...) custom-call(s32[14]{0:T(128)S(1)} %get-tuple-element.76.meta, ...), custom_call_target="tpu_custom_call" | custom-call | tf_op jit(solution)/shard_map/cond/branch_1_fun/finish/pallas_call | solution.py:1664
Async XLA Ops:
  0.6 140.4 %copy-start = (bf16[2,512,1536]{2,1,0:T(8,128)(2,1)S(1)}, bf16[2,512,1536]{2,1,0:T(8,128)(2,1)}, u32[]{:S(2)}) copy-start(bf16[2,512,1536]{2,1,0:T(8,128)(2,1)} %w_qkv.1) | copy-start | bytes 9437188
  0.7 140.4 %copy-start.1 = (bf16[12,64,512]{2,1,0:T(8,128)(2,1)S(1)}, bf16[12,64,512]{2,1,0:T(8,128)(2,1)}, u32[]{:S(2)}) copy-start(bf16[12,64,512]{2,1,0:T(8,128)(2,1)} %cotangent.1) | copy-start | bytes 2359300
  0.7 140.4 %copy-start.2 = (s32[12,256]{1,0:T(8,128)S(1)}, s32[12,256]{1,0:T(8,128)}, u32[]{:S(2)}) copy-start(s32[12,256]{1,0:T(8,128)} %row_index.1) | copy-start | bytes 36868
  0.7 140.4 %copy-start.3 = (f32[2,2,512]{2,1,0:T(2,128)S(1)}, f32[2,2,512]{2,1,0:T(2,128)}, u32[]{:S(2)}) copy-start(f32[2,2,512]{2,1,0:T(2,128)} %gain.1) | copy-start | bytes 24580
  0.7 140.4 %copy-start.4 = (f32[2,2048]{1,0:T(2,128)S(1)}, f32[2,2048]{1,0:T(2,128)}, u32[]{:S(2)}) copy-start(f32[2,2048]{1,0:T(2,128)} %bias_in.1) | copy-start | bytes 49156
  0.7 140.4 %copy-start.5 = (f32[2,1024]{1,0:T(2,128)S(1)}, f32[2,1024]{1,0:T(2,128)}, u32[]{:S(2)}) copy-start(f32[2,1024]{1,0:T(2,128)} %bias_qv.1) | copy-start | bytes 24580
  0.7 140.4 %copy-start.6 = (f32[2,2,512]{2,1,0:T(2,128)S(1)}, f32[2,2,512]{2,1,0:T(2,128)}, u32[]{:S(2)}) copy-start(f32[2,2,512]{2,1,0:T(2,128)} %out_bias.1) | copy-start | bytes 24580
  0.7 140.4 %copy-start.7 = (f32[2,2,512]{2,1,0:T(2,128)S(1)}, f32[2,2,512]{2,1,0:T(2,128)}, u32[]{:S(2)}) copy-start(f32[2,2,512]{2,1,0:T(2,128)} %shift.1) | copy-start | bytes 24580
  0.7 140.4 %copy-start.8 = (s32[12]{0:T(128)S(1)}, s32[12]{0:T(128)}, u32[]{:S(2)}) copy-start(s32[12]{0:T(128)} %windows.1) | copy-start | bytes 148
where the time goes:
time: 148 us
  Pallas kernels  145 us (98%)
  between operations  1.63 us (1%)
    pallas_call x1, Pallas kernels, packed_way(): pl.pallas_call(functools.partial(packed_kernel, owners, size), name='pack...  139 us
    pallas_call x1, Pallas kernels, finish(): pl.pallas_call(functools.partial(finish_kernel, at_var), name='finish', o...  6.37 us

commit v1 on v0

--- a/solution.py
+++ b/solution.py
@@ -16,7 +16,8 @@
 F32 = jnp.float32
 MESH = pl.DeviceIdType.MESH
 VMEM_BYTES = 60 << 20
-PACKED = 448
+BLOCKS = (256, 224)
+PACKED = sum(BLOCKS)
 SMOOTH = 0.7978845608028654
 CUBIC = 0.044715
 
@@ -326,31 +327,10 @@
         for low in range(stop):
             first, second = keys[low], keys[low + 1]
             keys[low], keys[low + 1] = jnp.maximum(first, second), jnp.minimum(first, second)
-    load = [jnp.int32(0)] * owners
-    held = [jnp.int32(0)] * owners
-    slots, names = [], []
-    for key in keys:
-        count, name = key // wins, lax.rem(key, wins)
-        best, which = load[0] + (held[0] // each) * 1000000, jnp.int32(0)
-        for owner in range(1, owners):
-            price = load[owner] + (held[owner] // each) * 1000000
-            better = price < best
-            best = jnp.where(better, price, best)
-            which = jnp.where(better, owner, which)
-        slot = jnp.int32(0)
-        for owner in range(owners):
-            mine = which == owner
-            slot = jnp.where(mine, owner * each + held[owner], slot)
-            load[owner] = jnp.where(mine, load[owner] + ((count + 15) // 16) * 16, load[owner])
-            held[owner] = jnp.where(mine, held[owner] + 1, held[owner])
-        slots.append(slot)
-        names.append(name)
+    names = [lax.rem(key, wins) for key in keys]
     order = []
-    for place in range(wins):
-        window = jnp.int32(0)
-        for slot, name in zip(slots, names):
-            window = jnp.where(slot == place, name, window)
-        order.append(window)
+    for owner in range(owners):
+        order += [names[owner], names[2 * owners - 1 - owner], names[2 * owners + owner]]
     return order
 
 
@@ -1223,9 +1203,8 @@
         names.append(name)
         counts.append(windows[name])
 
-    starts = [jnp.int32(0)]
-    for count in counts:
-        starts.append(starts[-1] + count)
+    shares = counts[0] + counts[2] <= BLOCKS[0]
+    starts = [jnp.int32(0), jnp.int32(BLOCKS[0]), jnp.where(shares, counts[0], BLOCKS[0] + counts[1])]
     for place in range(each):
         hits = marks(row_index, names[place], counts[place], length)
         along = lax.broadcasted_iota(jnp.int32, (length, size), 0) + starts[place]
@@ -1234,20 +1213,19 @@
 
     row = lax.broadcasted_iota(jnp.int32, (size, 128), 0)
     lane = lax.broadcasted_iota(jnp.int32, (size, 128), 1)
-    owner = jnp.zeros((size, 128), jnp.int32)
-    for start in starts[1:]:
-        owner = owner + jnp.where(row >= start, 1, 0)
+    owner = jnp.full((size, 128), each, jnp.int32)
+    for place in range(each):
+        inside = jnp.logical_and(row >= starts[place], row < starts[place] + counts[place])
+        owner = jnp.where(inside, place, owner)
     key_mark = jnp.where(lane == owner, 1.0, 0.0).astype(LOW)
     query_mark = jnp.where(lane == owner, jnp.where(lane < each, 0.0, -1e30), -1e30).astype(LOW)
-    query_mark = jnp.concatenate([query_mark, query_mark], axis=0)
     lane_low, lane_high = lane_masks(128)
 
     largest = jnp.int32(0)
     for owner in range(owners):
-        total = jnp.int32(0)
-        for place in range(each):
-            total = total + windows[order[owner * each + place]]
-        largest = jnp.maximum(largest, total)
+        held = [windows[order[owner * each + place]] for place in range(each)]
+        second = jnp.where(held[0] + held[2] <= BLOCKS[0], held[1], held[1] + held[2])
+        largest = jnp.maximum(largest, second)
     most[0] = jnp.full(most.shape[1:], largest, jnp.int32)
     for turn, friend in enumerate(across):
         copy = pltpu.make_async_remote_copy(
@@ -1269,12 +1247,18 @@
     state[...] = dot(spots[...], x[...].reshape(each * length, width), 0, 0)
     fetch(0, 0).wait()
 
-    def masked_scores(layer, at):
-        query = two_heads(qkv[layer, :, pl.ds(at, 128)], lane_low, lane_high)
-        key = qkv[layer, :, pl.ds(at + width, 128)]
-        value = qkv[layer, :, pl.ds(at + 2 * width, 128)]
+    spans = []
+    for block in BLOCKS:
+        first = spans[-1].stop if spans else 0
+        spans.append(slice(first, first + block))
+
+    def masked_scores(layer, at, span):
+        query = two_heads(qkv[layer, span, pl.ds(at, 128)], lane_low, lane_high)
+        key = qkv[layer, span, pl.ds(at + width, 128)]
+        value = qkv[layer, span, pl.ds(at + 2 * width, 128)]
+        allowed = jnp.concatenate([query_mark[span], query_mark[span]], axis=0)
         scores = dot(
-            jnp.concatenate([key, key_mark], axis=1), jnp.concatenate([query, query_mark], axis=1), 1, 1
+            jnp.concatenate([key, key_mark[span]], axis=1), jnp.concatenate([query, allowed], axis=1), 1, 1
         )
         return query, key, value, scores
 
@@ -1295,20 +1279,20 @@
             else:
                 joint = joint.astype(LOW)
             qkv[layer, :, columns] = joint
-        for pair in range(pairs):
+        for pair, span in [(pair, span) for pair in range(pairs) for span in spans]:
             at = pair * 128
-            _, _, value, scores = masked_scores(layer, at)
+            _, _, value, scores = masked_scores(layer, at, span)
             peak = jnp.max(scores, axis=0, keepdims=True)
             expo = jnp.exp(scores - peak)
             total = jnp.sum(expo, axis=0, keepdims=True)
             probs = (expo * (1.0 / total)).astype(LOW)
-            lefts[layer, 1, :, pl.ds(at, 128)] = join_heads(dot(probs, value, 0, 0)).astype(LOW)
-            top[layer, pair] = peak + jnp.log(total)
+            lefts[layer, 1, span, pl.ds(at, 128)] = join_heads(dot(probs, value, 0, 0)).astype(LOW)
+            top[layer, pair, :, 2 * span.start : 2 * span.stop] = peak + jnp.log(total)
         for which in range(1, 4):
             fetch(layer, which).wait()
         first = dot(lefts[layer, 1], wv_attn[layer], 1, 0) + out_bias[layer, 0:1, :]
         one, inverse_one = normalize(state[...] + first)
-        normal[layer, 0] = one
+        normal[layer, 0] = one.astype(LOW)
         after = one * gain[layer, 0:1, :] + shift[layer, 0:1, :]
         after_low = after.astype(LOW)
         lefts[layer, 2] = after_low
@@ -1328,7 +1312,7 @@
                 ]
             second = second + dot(active, wv_out[layer, columns, :], 1, 0)
         two, inverse_two = normalize(after + second + out_bias[layer, 1:2, :])
-        normal[layer, 1] = two
+        normal[layer, 1] = two.astype(LOW)
         state[...] = two * gain[layer, 1:2, :] + shift[layer, 1:2, :]
         lanes = lax.broadcasted_iota(jnp.int32, (size, 128), 1)
         inverse[layer] = jnp.where(lanes < 64, inverse_one, inverse_two)
@@ -1358,7 +1342,7 @@
             net.take(1, first + place)
 
         grad = state[...]
-        two = normal[layer, 1]
+        two = normal[layer, 1].astype(F32)
         back = normalize_back(grad, gain[layer, 1:2, :], two, inverse[layer, :, 64:65])
         back_low = back.astype(LOW)
         last_right[...] = back_low
@@ -1372,7 +1356,7 @@
 
             return carry
 
-        lax.fori_loop(0, pieces, outer, 0)
+        lax.fori_loop(0, pieces, outer, 0, unroll=4)
         add_rows(layer, 9, grad * two)
         add_rows(layer, 11, grad)
         add_rows(layer, 3, back_low.astype(F32))
@@ -1396,7 +1380,7 @@
 
         lax.fori_loop(0, pieces, inner, 0)
         back = state[...]
-        one = normal[layer, 0]
+        one = normal[layer, 0].astype(F32)
         add_rows(layer, 8, back * one)
         add_rows(layer, 10, back)
         back = normalize_back(back, gain[layer, 0:1, :], one, inverse[layer, :, 0:1])
@@ -1407,18 +1391,18 @@
         mixed_grad[...] = dot(back_low, wv_attn[layer], 1, 1).astype(LOW)
         state[...] = back
         net.pump(turn + 3)
-        for pair in range(pairs):
+        for pair, span in [(pair, span) for pair in range(pairs) for span in spans]:
             at = pair * 128
-            query, key, value, scores = masked_scores(layer, at)
-            grads = two_heads(mixed_grad[:, pl.ds(at, 128)], lane_low, lane_high)
-            probs = jnp.exp(scores - top[layer, pair])
+            query, key, value, scores = masked_scores(layer, at, span)
+            grads = two_heads(mixed_grad[span, pl.ds(at, 128)], lane_low, lane_high)
+            probs = jnp.exp(scores - top[layer, pair, :, 2 * span.start : 2 * span.stop])
             d_probs = dot(value, grads, 1, 1)
             centre = jnp.sum(probs * d_probs, axis=0, keepdims=True)
             d_scores = (probs * (d_probs - centre)).astype(LOW)
             d_query = join_heads(dot(d_scores, key, 0, 0)) * 0.125
-            rights[0, :, pl.ds(at, 128)] = d_query.astype(LOW)
-            rights[1, :, pl.ds(at, 128)] = dot(d_scores, query, 1, 0).astype(LOW)
-            rights[2, :, pl.ds(at, 128)] = dot(probs.astype(LOW), grads, 1, 0).astype(LOW)
+            rights[0, span, pl.ds(at, 128)] = d_query.astype(LOW)
+            rights[1, span, pl.ds(at, 128)] = dot(d_scores, query, 1, 0).astype(LOW)
+            rights[2, span, pl.ds(at, 128)] = dot(probs.astype(LOW), grads, 1, 0).astype(LOW)
         take(8)
         net.pump(turn + 4)
 
@@ -1431,7 +1415,7 @@
 
             return carry
 
-        lax.fori_loop(0, 3, last, 0)
+        lax.fori_loop(0, 3, last, 0, unroll=3)
         net.pump(turn + 5)
         grad = state[...]
         for which in range(3):
@@ -1715,7 +1699,7 @@
                 pltpu.VMEM((3, size, width), LOW),
                 pltpu.VMEM((layers, size, 3 * width), LOW),
                 pltpu.VMEM((layers, size, hidden_width), LOW),
-                pltpu.VMEM((layers, 2, size, width), F32),
+                pltpu.VMEM((layers, 2, size, width), LOW),
                 pltpu.VMEM((layers, size, 128), F32),
                 pltpu.VMEM((layers, width // 128, 1, 2 * size), F32),
                 pltpu.VMEM((size, width), LOW),
@@ -1840,7 +1824,7 @@
         return finish(wins + 2 * each, meta, merged, sums, layer_back, grad_back)
 
     *sums_up, order = packed_way()
-    return lax.cond(order[wins + 1] <= PACKED, lambda: finish(wins, order, *sums_up), ragged_way)
+    return lax.cond(order[wins + 1] <= BLOCKS[1], lambda: finish(wins, order, *sums_up), ragged_way)
 
 
 def choose(*arrays):

time: 148 us -> 144 us (0.973)
  Pallas kernels: 145 us -> 142 us
    pallas_call x1, Pallas kernels: 139 us -> 135 us  [packed_way(): pl.pallas_call(functools.partial(packed_kernel, owners, size), name='pack...]
where the time goes in v1:
time: 144 us
  Pallas kernels  142 us (99%)
  between operations  1.63 us (1%)
    pallas_call x1, Pallas kernels, packed_way(): pl.pallas_call(functools.partial(packed_kernel, owners, size), name='pack...  135 us
    pallas_call x1, Pallas kernels, finish(): pl.pallas_call(functools.partial(finish_kernel, at_var), name='finish', o...  6.37 us

profile of v1, /device:TPU:0, one launch (start us, length us, event | category | flops | bytes accessed | tf_op | source)
XLA Modules:
  0.0 143.8 jit_solution(14796490038517920710)
XLA Ops:
  0.6 0.0 copy-start
  0.7 0.0 copy-start.1
  0.7 0.0 copy-start.2
  0.7 0.0 copy-start.3
  0.7 0.0 copy-start.4
  0.7 0.0 copy-start.5
  0.7 0.0 copy-start.6
  0.7 0.0 copy-start.7
  0.7 0.0 copy-start.8
  0.7 135.1 %packed.1 = (bf16[24,128,512]{2,1,0:T(8,128)(2,1)}, f32[2,16,512]{2,1,0:T(8,128)S(1)}, bf16[12,64,512]{2,1,0:T(8,128)(2,1)}, bf16[12,64,512]{2,1,0:T(8,128)(2,1)}, s32[14]{0:T(128)S(1)}) custom-call(s32[12]{0:T(128)} %windows.1, s32[12,256]{1,0:T(8,128)} %row_index.1, bf16[12,64,512]{2,1,0:T(8,128)(2,1)} %inputs.1, bf16[12,64,512]{2,1,0:T(8,128)(2,1)} %cotangent.1, ...), custom_call_target="tpu_custom_call" | custom-call | tf_op jit(solution)/shard_map/packed/pallas_call | solution.py:1674
  135.9 0.6 slice.3
  137.1 0.0 copy-done
  137.1 0.0 copy-done.1
  137.1 0.0 copy-done.2
  137.2 0.0 copy-done.3
  137.2 0.0 copy-done.4
  137.2 0.0 copy-done.5
  137.2 0.0 copy-done.6
  137.2 0.0 copy-done.7
  137.2 0.0 copy-done.8
  137.2 6.4 %conditional.1 = (bf16[12,64,512]{2,1,0:T(8,128)(2,1)}, f32[12,64,512]{2,1,0:T(8,128)}, f32[2,128,1536]{2,1,0:T(8,128)}, f32[2,256]{1,0:T(2,128)}, f32[2,128,512...) conditional(s32[]{:T(128)} %bitcast, (s32[12]{0:T(128)S(1)}, ...), branch_computations={%region_0.0_spmd, %region_1.0_spmd} | conditional | bytes 88 | solution.py:1827
  137.2 6.4 %finish.3 = (bf16[12,64,512]{2,1,0:T(8,128)(2,1)}, f32[12,64,512]{2,1,0:T(8,128)}, f32[2,128,1536]{2,1,0:T(8,128)}, f32[2,128,512]{2,1,0:T(8,128)}, f32[2,128,20...) custom-call(s32[14]{0:T(128)S(1)} %get-tuple-element.76.meta, ...), custom_call_target="tpu_custom_call" | custom-call | tf_op jit(solution)/shard_map/cond/branch_1_fun/finish/pallas_call | solution.py:1648
Async XLA Ops:
  0.6 136.5 %copy-start = (bf16[2,512,1536]{2,1,0:T(8,128)(2,1)S(1)}, bf16[2,512,1536]{2,1,0:T(8,128)(2,1)}, u32[]{:S(2)}) copy-start(bf16[2,512,1536]{2,1,0:T(8,128)(2,1)} %w_qkv.1) | copy-start | bytes 9437188
  0.7 136.5 %copy-start.1 = (bf16[12,64,512]{2,1,0:T(8,128)(2,1)S(1)}, bf16[12,64,512]{2,1,0:T(8,128)(2,1)}, u32[]{:S(2)}) copy-start(bf16[12,64,512]{2,1,0:T(8,128)(2,1)} %cotangent.1) | copy-start | bytes 2359300
  0.7 136.5 %copy-start.2 = (s32[12,256]{1,0:T(8,128)S(1)}, s32[12,256]{1,0:T(8,128)}, u32[]{:S(2)}) copy-start(s32[12,256]{1,0:T(8,128)} %row_index.1) | copy-start | bytes 36868
  0.7 136.5 %copy-start.3 = (f32[2,2,512]{2,1,0:T(2,128)S(1)}, f32[2,2,512]{2,1,0:T(2,128)}, u32[]{:S(2)}) copy-start(f32[2,2,512]{2,1,0:T(2,128)} %gain.1) | copy-start | bytes 24580
  0.7 136.5 %copy-start.4 = (f32[2,2048]{1,0:T(2,128)S(1)}, f32[2,2048]{1,0:T(2,128)}, u32[]{:S(2)}) copy-start(f32[2,2048]{1,0:T(2,128)} %bias_in.1) | copy-start | bytes 49156
  0.7 136.5 %copy-start.5 = (f32[2,1024]{1,0:T(2,128)S(1)}, f32[2,1024]{1,0:T(2,128)}, u32[]{:S(2)}) copy-start(f32[2,1024]{1,0:T(2,128)} %bias_qv.1) | copy-start | bytes 24580
  0.7 136.5 %copy-start.6 = (f32[2,2,512]{2,1,0:T(2,128)S(1)}, f32[2,2,512]{2,1,0:T(2,128)}, u32[]{:S(2)}) copy-start(f32[2,2,512]{2,1,0:T(2,128)} %out_bias.1) | copy-start | bytes 24580
  0.7 136.5 %copy-start.7 = (f32[2,2,512]{2,1,0:T(2,128)S(1)}, f32[2,2,512]{2,1,0:T(2,128)}, u32[]{:S(2)}) copy-start(f32[2,2,512]{2,1,0:T(2,128)} %shift.1) | copy-start | bytes 24580
  0.7 136.5 %copy-start.8 = (s32[12]{0:T(128)S(1)}, s32[12]{0:T(128)}, u32[]{:S(2)}) copy-start(s32[12]{0:T(128)} %windows.1) | copy-start | bytes 148

commit v2 on v1

--- a/solution.py
+++ b/solution.py
@@ -975,7 +975,7 @@
 SETTLED = (2, 3, 4, 5, 6, 7, 8)
 LAG = 2
 DEPTH = 4
-Y_FIRST = (1, 7)
+Y_FIRST = (1,)
 Z_FIRST = (4, 10)
 
 
@@ -1111,14 +1111,12 @@
                 def _():
                     self.exchange(1, turn + DEPTH).start()
 
-    def settle(self):
-        def one(chunk, carry):
-            for stage in range(1, 8):
-                self.exchange(stage, chunk).wait_send()
-            self.out_copy(chunk).wait()
-            return carry
-
-        lax.fori_loop(0, self.chunks, one, 0)
+    def settle(self, chunk):
+        for stage in range(1, 8):
+            self.exchange(stage, chunk).wait_send()
+        self.out_copy(chunk).wait()
+
+    def settle_ring(self):
         for chunk in range(self.chunks - self.ring, self.chunks):
             self.exchange(0, chunk).wait_send()
 
@@ -1240,10 +1238,14 @@
         copy.wait()
         most[turn + 1] = jnp.maximum(most[turn], most_got[turn])
     meta[wins + 1] = jnp.max(most[len(across)])
-    for copy in to_owners(x_stage, x, 3):
-        copy.wait()
+    *away, home = to_owners(x_stage, x, 3)
+    for copy in away:
+        copy.wait_send()
     for copy in to_owners(g_stage, g, 0):
         copy.start()
+    for copy in away:
+        copy.wait_recv()
+    home.wait()
     state[...] = dot(spots[...], x[...].reshape(each * length, width), 0, 0)
     fetch(0, 0).wait()
 
@@ -1430,6 +1432,7 @@
 
     lax.fori_loop(0, layers, backward_layer, 0)
     first_turn = 7 * layers
+    settled = LAG * (len(SETTLED) - 1) + 1
     grad_out[...] = dot(spots[...], state[...].astype(LOW), 1, 0).astype(LOW).reshape(grad_out.shape)
 
     route = [partner(axis, bit) for axis, bit in ROUTE]
@@ -1449,6 +1452,7 @@
 
     def step(now, carry):
         net.pump(now)
+        net.settle(now - settled)
 
         @pl.when(now == net.chunks - 1)
         def _():
@@ -1470,7 +1474,9 @@
         return carry
 
     lax.fori_loop(first_turn, net.chunks + LAG * (len(SETTLED) - 1), step, 0)
-    net.settle()
+    for chunk in [*range(first_turn - settled), *range(net.chunks - 1, net.chunks)]:
+        net.settle(chunk)
+    net.settle_ring()
     for place in range(5):
         sums_exchange(place).wait_send()
     for copy in to_slots(layer_out, layer_back, 1) + to_slots(grad_out, grad_back, 2):

time: 144 us -> 144 us (level)
  no operation moved by 1% of the time
where the time goes in v2:
time: 144 us
  Pallas kernels  141 us (98%)
  between operations  1.63 us (1%)
    pallas_call x1, Pallas kernels, packed_way(): pl.pallas_call(functools.partial(packed_kernel, owners, size), name='pack...  135 us
    pallas_call x1, Pallas kernels, finish(): pl.pallas_call(functools.partial(finish_kernel, at_var), name='finish', o...  6.37 us

profile of v2, /device:TPU:0, one launch (start us, length us, event | category | flops | bytes accessed | tf_op | source)
XLA Modules:
  0.0 143.6 jit_solution(1404658921722670468)
XLA Ops:
  0.6 0.0 copy-start
  0.7 0.0 copy-start.1
  0.7 0.0 copy-start.2
  0.7 0.0 copy-start.3
  0.7 0.0 copy-start.4
  0.7 0.0 copy-start.5
  0.7 0.0 copy-start.6
  0.7 0.0 copy-start.7
  0.7 0.0 copy-start.8
  0.7 134.9 %packed.1 = (bf16[24,128,512]{2,1,0:T(8,128)(2,1)}, f32[2,16,512]{2,1,0:T(8,128)S(1)}, bf16[12,64,512]{2,1,0:T(8,128)(2,1)}, bf16[12,64,512]{2,1,0:T(8,128)(2,1)}, s32[14]{0:T(128)S(1)}) custom-call(s32[12]{0:T(128)} %windows.1, s32[12,256]{1,0:T(8,128)} %row_index.1, bf16[12,64,512]{2,1,0:T(8,128)(2,1)} %inputs.1, bf16[12,64,512]{2,1,0:T(8,128)(2,1)} %cotangent.1, ...), custom_call_target="tpu_custom_call" | custom-call | tf_op jit(solution)/shard_map/packed/pallas_call | solution.py:1680
  135.7 0.6 slice.3
  136.9 0.0 copy-done
  136.9 0.0 copy-done.1
  136.9 0.0 copy-done.2
  137.0 0.0 copy-done.3
  137.0 0.0 copy-done.4
  137.0 0.0 copy-done.5
  137.0 0.0 copy-done.6
  137.0 0.0 copy-done.7
  137.0 0.0 copy-done.8
  137.0 6.4 %conditional.1 = (bf16[12,64,512]{2,1,0:T(8,128)(2,1)}, f32[12,64,512]{2,1,0:T(8,128)}, f32[2,128,1536]{2,1,0:T(8,128)}, f32[2,256]{1,0:T(2,128)}, f32[2,128,512...) conditional(s32[]{:T(128)} %bitcast, (s32[12]{0:T(128)S(1)}, ...), branch_computations={%region_0.0_spmd, %region_1.0_spmd} | conditional | bytes 88 | solution.py:1833
  137.0 6.4 %finish.3 = (bf16[12,64,512]{2,1,0:T(8,128)(2,1)}, f32[12,64,512]{2,1,0:T(8,128)}, f32[2,128,1536]{2,1,0:T(8,128)}, f32[2,128,512]{2,1,0:T(8,128)}, f32[2,128,20...) custom-call(s32[14]{0:T(128)S(1)} %get-tuple-element.76.meta, ...), custom_call_target="tpu_custom_call" | custom-call | tf_op jit(solution)/shard_map/cond/branch_1_fun/finish/pallas_call | solution.py:1654
Async XLA Ops:
  0.6 136.3 %copy-start = (bf16[2,512,1536]{2,1,0:T(8,128)(2,1)S(1)}, bf16[2,512,1536]{2,1,0:T(8,128)(2,1)}, u32[]{:S(2)}) copy-start(bf16[2,512,1536]{2,1,0:T(8,128)(2,1)} %w_qkv.1) | copy-start | bytes 9437188
  0.7 136.3 %copy-start.1 = (bf16[12,64,512]{2,1,0:T(8,128)(2,1)S(1)}, bf16[12,64,512]{2,1,0:T(8,128)(2,1)}, u32[]{:S(2)}) copy-start(bf16[12,64,512]{2,1,0:T(8,128)(2,1)} %cotangent.1) | copy-start | bytes 2359300
  0.7 136.3 %copy-start.2 = (s32[12,256]{1,0:T(8,128)S(1)}, s32[12,256]{1,0:T(8,128)}, u32[]{:S(2)}) copy-start(s32[12,256]{1,0:T(8,128)} %row_index.1) | copy-start | bytes 36868
  0.7 136.3 %copy-start.3 = (f32[2,2,512]{2,1,0:T(2,128)S(1)}, f32[2,2,512]{2,1,0:T(2,128)}, u32[]{:S(2)}) copy-start(f32[2,2,512]{2,1,0:T(2,128)} %gain.1) | copy-start | bytes 24580
  0.7 136.3 %copy-start.4 = (f32[2,2048]{1,0:T(2,128)S(1)}, f32[2,2048]{1,0:T(2,128)}, u32[]{:S(2)}) copy-start(f32[2,2048]{1,0:T(2,128)} %bias_in.1) | copy-start | bytes 49156
  0.7 136.3 %copy-start.5 = (f32[2,1024]{1,0:T(2,128)S(1)}, f32[2,1024]{1,0:T(2,128)}, u32[]{:S(2)}) copy-start(f32[2,1024]{1,0:T(2,128)} %bias_qv.1) | copy-start | bytes 24580
  0.7 136.3 %copy-start.6 = (f32[2,2,512]{2,1,0:T(2,128)S(1)}, f32[2,2,512]{2,1,0:T(2,128)}, u32[]{:S(2)}) copy-start(f32[2,2,512]{2,1,0:T(2,128)} %out_bias.1) | copy-start | bytes 24580
  0.7 136.3 %copy-start.7 = (f32[2,2,512]{2,1,0:T(2,128)S(1)}, f32[2,2,512]{2,1,0:T(2,128)}, u32[]{:S(2)}) copy-start(f32[2,2,512]{2,1,0:T(2,128)} %shift.1) | copy-start | bytes 24580
  0.7 136.3 %copy-start.8 = (s32[12]{0:T(128)S(1)}, s32[12]{0:T(128)}, u32[]{:S(2)}) copy-start(s32[12]{0:T(128)} %windows.1) | copy-start | bytes 148
